TPU v7x, 256 devices: a whole 4x4x8 slice. The times are simulated.
256 devices in a mesh: view: 16 (over y, z_hi), row: 16 (over z_lo, x, core).
Axes of the slice: x: 4, y: 4, z: 8 (z_hi: 4, z_lo: 2; z = z_hi * 2 + z_lo), core: 2. Of those that a mesh axis runs over, the one named last changes fastest.
Arguments:
- stream_in: bfloat16 [16, 16, 128, 2048], P('view', 'row'), may hold values from -6 to 6
- query_in: bfloat16 [16, 16, 128, 2048], P('view', 'row'), may hold values from -240 to 240
- key_in: bfloat16 [16, 16, 128, 2048], P('view', 'row'), may hold values from -8 to 8
- value_in: bfloat16 [16, 16, 128, 2048], P('view', 'row'), may hold values from -6 to 6
- out_weight: bfloat16 [2048, 2048], P('view'), may hold values from -0.5 to 0.5
- norm_gain: float32 [2048], replicated, may hold values from 0.1 to 1.9
- up_weight: bfloat16 [2048, 4096], P(None, 'view'), may hold values from -0.125 to 0.125
- conv_taps: float32 [3, 3, 4096], P(None, None, 'view'), may hold values from -2 to 2
- down_weight: bfloat16 [4096, 2048], P('view'), may hold values from -0.1875 to 0.1875
Outputs:
- result: bfloat16 [16, 16, 128, 2048], P('view', 'row')
All inputs are finite; a program needn't handle non-finite values.
Results may differ from a plain program's by a relative error of at most 0.025.
Values may be sent and summed in bfloat16 or wider, within the bound.
No kernel may reach another device: no remote copies, remote signals or barrier semaphores. Data moves between devices by JAX's collectives and lax.ppermute only.
A program may use at most 64 MiB of HBM per device.

v0:
```python
import math

import jax
import jax.numpy as jnp
from jax import lax
from jax.sharding import PartitionSpec as P

HD = 128


def with_halo(cells, sides, width):
    for axis, dim in sides:
        count = lax.axis_size(axis)
        ends = count - 1
        head = lax.slice_in_dim(cells, 0, width, axis=dim)
        tail = lax.slice_in_dim(cells, cells.shape[dim] - width, cells.shape[dim], axis=dim)
        cells = jnp.concatenate(
            [
                lax.ppermute(tail, axis, [(i, (i + 1) % count) for i in range(ends)]),
                cells,
                lax.ppermute(head, axis, [((i + 1) % count, i) for i in range(ends)]),
            ],
            axis=dim,
        )
    return cells


def attend_rows(triple):
    query_all, key_all, value_all = triple
    view_count, row_count, col_count, heads_here, head_size = query_all.shape
    key_count = view_count * col_count
    block_size = math.gcd(512, key_count)
    scaling = 1.0 / math.sqrt(head_size)

    def flatten(array):
        return jnp.moveaxis(array, 1, 0).reshape(row_count, key_count, heads_here, head_size)

    def one_row(inputs):
        query_one, key_one, value_one = inputs

        def one_block(query_block):
            scores = (
                jnp.einsum("qhd,khd->hqk", query_block, key_one, preferred_element_type=jnp.float32)
                * scaling
            )
            weights = jax.nn.softmax(scores, axis=-1).astype(jnp.bfloat16)
            return jnp.einsum(
                "hqk,khd->qhd", weights, value_one, preferred_element_type=jnp.float32
            ).astype(jnp.bfloat16)

        blocks = query_one.reshape(key_count // block_size, block_size, heads_here, head_size)
        return lax.map(one_block, blocks).reshape(key_count, heads_here, head_size)

    attended = lax.map(one_row, (flatten(query_all), flatten(key_all), flatten(value_all)))
    attended = attended.reshape(row_count, view_count, col_count, heads_here, head_size)
    return jnp.moveaxis(attended, 0, 1)


def body(
    stream_in, query_in, key_in, value_in, out_weight, norm_gain, up_weight, conv_taps, down_weight
):
    lead_count, row_count, col_count, model_dim = stream_in.shape
    head_count = model_dim // HD

    def split_heads(array):
        return array.reshape(lead_count, row_count, col_count, head_count, HD)

    attended = attend_rows(
        (
            lax.all_to_all(split_heads(query_in), "view", split_axis=3, concat_axis=0, tiled=True),
            lax.all_to_all(split_heads(key_in), "view", split_axis=3, concat_axis=0, tiled=True),
            lax.all_to_all(split_heads(value_in), "view", split_axis=3, concat_axis=0, tiled=True),
        )
    )
    view_count = attended.shape[0]
    group_size = out_weight.shape[0]
    flat_heads = attended.reshape(view_count, row_count, col_count, group_size)
    picked = flat_heads
    product = jnp.dot(
        picked.reshape(-1, group_size), out_weight, preferred_element_type=jnp.float32
    )
    mixed = lax.psum_scatter(
        product.reshape(lead_count * lax.axis_size("view"), row_count, col_count, model_dim).astype(
            jnp.bfloat16
        ),
        "view",
        scatter_dimension=0,
        tiled=True,
    ).astype(jnp.float32)
    stream = stream_in.astype(jnp.float32) + mixed
    normed = (
        stream * lax.rsqrt(jnp.mean(stream * stream, axis=-1, keepdims=True) + 1e-06) * norm_gain
    ).astype(jnp.bfloat16)
    hidden_size = up_weight.shape[1]
    piece = lax.all_gather(normed, "view", axis=0, tiled=True)
    product = jnp.dot(piece.reshape(-1, model_dim), up_weight, preferred_element_type=jnp.float32)
    up_proj = product.astype(jnp.bfloat16).reshape(
        piece.shape[0], row_count, col_count, hidden_size
    )
    rimmed = with_halo(up_proj, (("row", 1),), 1)
    padded = jnp.pad(rimmed.astype(jnp.float32), ((0, 0), (0, 0), (1, 1), (0, 0)))
    conv_sum = jnp.zeros((view_count, row_count, col_count, hidden_size), jnp.float32)
    for offset_row in range(3):
        for offset_col in range(3):
            conv_sum = (
                conv_sum
                + conv_taps[offset_row, offset_col]
                * padded[
                    :, offset_row : offset_row + row_count, offset_col : offset_col + col_count, :
                ]
            )
    activated = jax.nn.gelu(conv_sum).astype(jnp.bfloat16)
    picked = activated
    product = jnp.dot(
        picked.reshape(-1, hidden_size), down_weight, preferred_element_type=jnp.float32
    )
    feed = lax.psum_scatter(
        product.reshape(lead_count * lax.axis_size("view"), row_count, col_count, model_dim).astype(
            jnp.bfloat16
        ),
        "view",
        scatter_dimension=0,
        tiled=True,
    ).astype(jnp.float32)
    return (stream + feed).astype(jnp.bfloat16)


def solution(mesh):
    return jax.shard_map(
        body,
        mesh=mesh,
        in_specs=(
            P("view", "row", None, None),
            P("view", "row", None, None),
            P("view", "row", None, None),
            P("view", "row", None, None),
            P("view", None),
            P(),
            P(None, "view"),
            P(None, None, "view"),
            P("view", None),
        ),
        out_specs=P("view", "row", None, None),
        check_vma=False,
    )
```

profile of v0, /device:TPU:1, one launch (start us, length us, event | category | flops | bytes accessed | tf_op | source)
XLA Modules:
  0.0 498.6 jit_solution(14381958632670187560)
XLA Ops:
  6.5 2.2 copy.28
  8.7 11.7 %all-to-all-start = ((bf16[1,1,128,16,128]{2,4,1,0,3:T(8,128)(2,1)}), bf16[1,1,128,16,128]{2,4,1,0,3:T(8,128)(2,1)S(1)}, u32[]{:S(2)}, u32[]{:S(2)}) async-start(bf16[1,1,128,16,128]{2,4,1,0,3:T(8,128)(2,1)} %bitcast.9), calls=%async_computation | async-start | bytes 1048576 | tf_op jit(solution)/shard_map/all_to_all | solution.py:70
  20.5 1.0 copy.31
  21.5 15.3 %all-to-all-done = bf16[1,1,128,16,128]{2,4,1,0,3:T(8,128)(2,1)S(1)} async-done(((bf16[1,1,128,16,128]{2,4,1,0,3:T(8,128)(2,1)}), bf16[1,1,128,16,128]{2,4,1,0,3:T(8,128)(2,1)S(1)}, u32[]{:S(2)}, u32[]{:S(2)}) %all-to-all-start) | async-done | bytes 524320 | tf_op jit(solution)/shard_map/all_to_all | solution.py:70
  36.8 5.0 %all-to-all-start.1 = ((bf16[1,1,128,16,128]{2,4,1,0,3:T(8,128)(2,1)}), bf16[1,1,128,16,128]{2,4,1,0,3:T(8,128)(2,1)S(1)}, u32[]{:S(2)}, u32[]{:S(2)}) async-start(bf16[1,1,128,16,128]{2,4,1,0,3:T(8,128)(2,1)} %bitcast.15), calls=%async_computation.1 | async-start | bytes 1048576 | tf_op jit(solution)/shard_map/all_to_all | solution.py:71
  41.8 1.0 copy.34
  42.8 16.2 %all-to-all-done.1 = bf16[1,1,128,16,128]{2,4,1,0,3:T(8,128)(2,1)S(1)} async-done(((bf16[1,1,128,16,128]{2,4,1,0,3:T(8,128)(2,1)}), bf16[1,1,128,16,128]{2,4,1,0,3:T(8,128)(2,1)S(1)}, u32[]{:S(2)}, u32[]{:S(2)}) %all-to-all-start.1) | async-done | bytes 524320 | tf_op jit(solution)/shard_map/all_to_all | solution.py:71
  59.0 4.0 all-to-all-start.2
  63.7 16.7 %all-to-all-done.2 = bf16[1,1,128,16,128]{2,4,1,0,3:T(8,128)(2,1)S(1)} async-done(((bf16[1,1,128,16,128]{2,4,1,0,3:T(8,128)(2,1)}), bf16[1,1,128,16,128]{2,4,1,0,3:T(8,128)(2,1)S(1)}, u32[]{:S(2)}, u32[]{:S(2)}) %all-to-all-start.2) | async-done | bytes 524320 | tf_op jit(solution)/shard_map/all_to_all | solution.py:72
  80.3 1.0 copy.36
  81.3 13.9 %while.17 = (s32[]{:T(128)}, bf16[4,512,1,128]{3,1,2,0:T(8,128)(2,1)}, bf16[4,512,1,128]{3,1,2,0:T(8,128)(2,1)S(1)}, bf16[2048,1,128]{2,0,1:T(8,128)(2,1)S(1)}, bf16[2048,1,128]{2,0,1:T(8,128)(2,1)}, /*index=5*/s32[]{:T(128)}) while((s32[]{:T(128)}, bf16[4,512,1,128]{3,1,2,0:T(8,128)(2,1)}, bf16[4,512,1,128]{3,1,2,0:T(8,128)(2,1)S(1)}, ...), condition=%wide.region_3.0_spmd, body=%wide.region_0.3_spmd.sunk | while | flops 546372608 | bytes 16001137 | solution.py:52
  82.1 0.8 fusion.53
  83.2 1.7 fusion.54
  85.6 0.8 fusion.53
  86.7 1.7 fusion.54
  89.1 0.8 fusion.53
  90.1 1.7 fusion.54
  92.6 0.8 fusion.53
  93.6 1.7 fusion.54
  95.3 6.6 %convert_bitcast_fusion.1 = bf16[16,1,128,2048]{3,2,0,1:T(8,128)(2,1)} fusion(bf16[16,128,128]{2,1,0:T(8,128)(2,1)} %bitcast.98, bf16[128,2048]{1,0:T(8,128)(2,1)S(1)} %copy-done.3), kind=kOutput, calls=%fused_computation.16 | convolution fusion | flops 1077936128 | bytes 9437184 | tf_op jit(solution)/shard_map/dot_general | solution.py:79
  102.0 116.6 %reduce-scatter.3.cloned.1.call-done = bf16[1,1,128,2048]{3,2,0,1:T(8,128)(2,1)} async-done(((bf16[16,1,128,2048]{3,2,0,1:T(8,128)(2,1)}), bf16[1,1,128,2048]{3,2,0,1:T(8,128)(2,1)}) %reduce-scatter.3.cloned.1.call-update) | async-done | bytes 524304 | tf_op jit(solution)/shard_map/reduce_scatter | solution.py:82
  218.6 1.3 multiply_reduce_fusion.1
  219.9 2.0 fusion.37
  222.0 103.1 %all-gather.2.cloned.1.call-done = bf16[16,1,128,2048]{3,2,1,0:T(8,128)(2,1)} async-done(((bf16[1,1,128,2048]{3,2,1,0:T(8,128)(2,1)}), bf16[16,1,128,2048]{3,2,1,0:T(8,128)(2,1)}) %all-gather.2.cloned.1.call-update) | async-done | bytes 8388624 | tf_op jit(solution)/shard_map/all_gather | solution.py:95
  325.1 5.7 %convolution_convert_fusion = bf16[2048,256]{1,0:T(8,128)(2,1)S(1)} fusion(bf16[2048,2048]{1,0:T(8,128)(2,1)} %bitcast.109, bf16[2048,256]{1,0:T(8,128)(2,1)S(1)} %copy-done.9), kind=kOutput, calls=%fused_computation.25 | convolution fusion | flops 2148007936 | bytes 10485760 | tf_op jit(solution)/shard_map/dot_general | solution.py:96
  330.8 2.6 collective-permute-start.1
  333.4 3.2 collective-permute-start
  336.6 10.3 %collective-permute-done.1 = bf16[16,1,128,256]{3,2,0,1:T(8,128)(2,1)S(1)} collective-permute-done((bf16[16,1,128,256]{3,2,0,1:T(8,128)(2,1)S(1)}, bf16[16,1,128,256]{3,2,0,1:T(8,128)(2,1)S(1)}, u32[]{:S(2)}, u32[]{:S(2)}) %collective-permute-start.1) | collective-permute-done | bytes 1048608 | tf_op jit(solution)/shard_map/ppermute | solution.py:21
  346.9 1.2 collective-permute-done
  348.6 6.8 %convert_bitcast_fusion = bf16[16,1,128,2048]{3,2,0,1:T(8,128)(2,1)} fusion(bf16[256,2048]{1,0:T(8,128)(2,1)S(1)} %copy-done, f32[16,3,128,256]{3,2,0,1:T(8,128)S(1)} %maximum_convert_fusion, f32[256]{0:T(256)S(1)} %bitcast.107, f32[256]{0:T(256)S(1)} %bitcast.108, f32[256]{0:T(256)S(1)} %bitcast.101, f32[256]{0:T(256)S(1)} %bitcast.102, ...), kind=kOutput, calls=%fused_computation.15 | convolution fusion | flops 2165309440 | bytes 22029312 | tf_op jit(solution)/shard_map/dot_general | solution.py:114
  355.4 134.5 %reduce-scatter.5.cloned.1.call-done = bf16[1,1,128,2048]{3,2,0,1:T(8,128)(2,1)} async-done(((bf16[16,1,128,2048]{3,2,0,1:T(8,128)(2,1)}), bf16[1,1,128,2048]{3,2,0,1:T(8,128)(2,1)}) %reduce-scatter.5.cloned.1.call-update) | async-done | bytes 524304 | tf_op jit(solution)/shard_map/reduce_scatter | solution.py:117
  490.0 2.1 fusion.38
  (42 shorter events, 5.3 us)
Async XLA Ops:
  6.5 342.1 %copy-start = (bf16[256,2048]{1,0:T(8,128)(2,1)S(1)}, bf16[256,2048]{1,0:T(8,128)(2,1)}, u32[]{:S(2)}) copy-start(bf16[256,2048]{1,0:T(8,128)(2,1)} %param.19) | copy-start | bytes 3145732
  6.5 14.0 %copy-start.4 = (bf16[1,1,128,2048]{3,2,1,0:T(8,128)(2,1)S(1)}, bf16[1,1,128,2048]{3,2,1,0:T(8,128)(2,1)}, u32[]{:S(2)}) copy-start(bf16[1,1,128,2048]{3,2,1,0:T(8,128)(2,1)} %param.13) | copy-start | bytes 1572868
  6.5 35.3 %copy-start.5 = (bf16[1,1,128,2048]{3,2,1,0:T(8,128)(2,1)S(1)}, bf16[1,1,128,2048]{3,2,1,0:T(8,128)(2,1)}, u32[]{:S(2)}) copy-start(bf16[1,1,128,2048]{3,2,1,0:T(8,128)(2,1)} %param.14) | copy-start | bytes 1572868
  8.7 28.0 %all-to-all-start = ((bf16[1,1,128,16,128]{2,4,1,0,3:T(8,128)(2,1)}), bf16[1,1,128,16,128]{2,4,1,0,3:T(8,128)(2,1)S(1)}, u32[]{:S(2)}, u32[]{:S(2)}) async-start(bf16[1,1,128,16,128]{2,4,1,0,3:T(8,128)(2,1)} %bitcast.9), calls=%async_computation | async-start | bytes 1048576 | tf_op jit(solution)/shard_map/all_to_all | solution.py:70
  36.8 22.2 %all-to-all-start.1 = ((bf16[1,1,128,16,128]{2,4,1,0,3:T(8,128)(2,1)}), bf16[1,1,128,16,128]{2,4,1,0,3:T(8,128)(2,1)S(1)}, u32[]{:S(2)}, u32[]{:S(2)}) async-start(bf16[1,1,128,16,128]{2,4,1,0,3:T(8,128)(2,1)} %bitcast.15), calls=%async_computation.1 | async-start | bytes 1048576 | tf_op jit(solution)/shard_map/all_to_all | solution.py:71
  59.0 21.3 %all-to-all-start.2 = ((bf16[1,1,128,16,128]{2,4,1,0,3:T(8,128)(2,1)}), bf16[1,1,128,16,128]{2,4,1,0,3:T(8,128)(2,1)S(1)}, u32[]{:S(2)}, u32[]{:S(2)}) async-start(bf16[1,1,128,16,128]{2,4,1,0,3:T(8,128)(2,1)} %bitcast.20), calls=%async_computation.2 | async-start | bytes 1048576 | tf_op jit(solution)/shard_map/all_to_all | solution.py:72
  63.0 155.5 %reduce-scatter.3.cloned.1.call-start = ((), (), s32[]{:S(2)}) async-start(), calls=%async_computation.5 | async-start | bytes 8912896 | tf_op jit(solution)/shard_map/reduce_scatter | solution.py:82
  81.3 14.0 %copy-start.3 = (bf16[128,2048]{1,0:T(8,128)(2,1)S(1)}, bf16[128,2048]{1,0:T(8,128)(2,1)}, u32[]{:S(2)}) copy-start(bf16[128,2048]{1,0:T(8,128)(2,1)} %param.15) | copy-start | bytes 1572868
  82.1 1.0 copy-start.6
  85.6 1.0 copy-start.6
  89.1 1.0 copy-start.6
  92.6 1.0 copy-start.6
  101.9 116.7 %copy-start.1 = (bf16[1,1,128,2048]{3,2,1,0:T(8,128)(2,1)S(1)}, bf16[1,1,128,2048]{3,2,1,0:T(8,128)(2,1)}, u32[]{:S(2)}) copy-start(bf16[1,1,128,2048]{3,2,1,0:T(8,128)(2,1)} %param.11) | copy-start | bytes 1572868
  101.9 118.0 %copy-start.7 = (f32[2048]{0:T(1024)S(1)}, f32[2048]{0:T(1024)}, u32[]{:S(2)}) copy-start(f32[2048]{0:T(1024)} %param.16) | copy-start | bytes 24580
  101.9 223.2 %copy-start.9 = (bf16[2048,256]{1,0:T(8,128)(2,1)S(1)}, bf16[2048,256]{1,0:T(8,128)(2,1)}, u32[]{:S(2)}) copy-start(bf16[2048,256]{1,0:T(8,128)(2,1)} %param.17) | copy-start | bytes 3145732
  101.9 223.1 %all-gather.2.cloned.1.call-start = ((), (), s32[]{:S(2)}) async-start(), calls=%async_computation.6 | async-start | bytes 8912896 | tf_op jit(solution)/shard_map/all_gather | solution.py:95
  221.9 268.0 %reduce-scatter.5.cloned.1.call-start = ((), (), s32[]{:S(2)}) async-start(), calls=%async_computation.7 | async-start | bytes 8912896 | tf_op jit(solution)/shard_map/reduce_scatter | solution.py:117
  325.1 11.5 %copy-start.8 = (f32[3,3,256]{2,1,0:T(4,128)S(1)}, f32[3,3,256]{2,1,0:T(4,128)}, u32[]{:S(2)}) copy-start(f32[3,3,256]{2,1,0:T(4,128)} %param.18) | copy-start | bytes 27652
  330.8 16.1 %collective-permute-start.1 = (bf16[16,1,128,256]{3,2,0,1:T(8,128)(2,1)S(1)}, bf16[16,1,128,256]{3,2,0,1:T(8,128)(2,1)S(1)}, u32[]{:S(2)}, u32[]{:S(2)}) collective-permute-start(bf16[16,1,128,256]{3,2,0,1:T(8,128)(2,1)S(1)} %bitcast.95), channel_id=1, source_target_pairs={{1,0},{2,1},{3,2},{4,3},{5,4},{6,5},{7,6},{8,7},{9,8},{10,9},{11,1... | collective-permute-start | bytes 3145736 | tf_op jit(solution)/shard_map/ppermute | solution.py:21
  333.4 14.7 %collective-permute-start = (bf16[16,1,128,256]{3,2,0,1:T(8,128)(2,1)S(1)}, bf16[16,1,128,256]{3,2,0,1:T(8,128)(2,1)S(1)}, u32[]{:S(2)}, u32[]{:S(2)}) collective-permute-start(bf16[16,1,128,256]{3,2,0,1:T(8,128)(2,1)S(1)} %bitcast.96), channel_id=1, source_target_pairs={{0,1},{1,2},{2,3},{3,4},{4,5},{5,6},{6,7},{7,8},{8,9},{9,10},{10,1... | collective-permute-start | bytes 3145736 | tf_op jit(solution)/shard_map/ppermute | solution.py:19
  355.4 134.5 %copy-start.2 = (bf16[1,1,128,2048]{3,2,0,1:T(8,128)(2,1)S(1)}, bf16[1,1,128,2048]{3,2,0,1:T(8,128)(2,1)}, u32[]{:S(2)}) copy-start(bf16[1,1,128,2048]{3,2,0,1:T(8,128)(2,1)} %reduce-scatter.3.cloned.1.call-done) | copy-start | bytes 1572868
Sparse Core Ops, SparseCore 0:
  102.0 116.4 reduce-scatter.2
  222.0 102.9 all-gather.1
  355.6 134.3 reduce-scatter.4
where the time goes:
time: 499 us
  waiting for transfers between devices  414 us (83%)
  matrix products  28.9 us (6%)
  starting transfers between devices  26.7 us (5%)
  between operations  13.2 us (3%)
  other arithmetic  9.18 us (2%)
  local copies, waits for them, and re-layouts  6.7 us (1%)
    reduce_scatter x2, waiting for transfers between devices, body(): lax.psum_scatter(product.reshape(lead_count * lax.axis_size('view'), row_...  251 us
    all_gather x1, waiting for transfers between devices, body(): piece = lax.all_gather(normed, 'view', axis=0, tiled=True)  103 us
    all_to_all x1, waiting for transfers between devices, body(): lax.all_to_all(split_heads(value_in), 'view', split_axis=3, concat_axis=0...  16.7 us
    all_to_all x1, waiting for transfers between devices, body(): lax.all_to_all(split_heads(key_in), 'view', split_axis=3, concat_axis=0,...  16.2 us
    all_to_all x1, waiting for transfers between devices, body(): lax.all_to_all(split_heads(query_in), 'view', split_axis=3, concat_axis=0...  15.3 us
    all_to_all x1, starting transfers between devices, body(): lax.all_to_all(split_heads(query_in), 'view', split_axis=3, concat_axis=0...  11.7 us
    ppermute x1, waiting for transfers between devices, with_halo(): lax.ppermute(head, axis, [((i + 1) % count, i) for i in range(ends)])  10.3 us
  transfers between devices with their start and end apart: 8, of which 8 were waited for; matrix products, arithmetic and copies ran while one was open for 1% of the time, Pallas kernels for 0%

commit v1 on v0

v1 whole, which is shorter than its diff:
```python
import math

import jax
import jax.numpy as jnp
from jax import lax
from jax.sharding import Mesh, PartitionSpec as P

HD = 128
VIEW = ("y", "zh")
ROW = ("zl", "x", "core")
NEAR = ("x", "core")


def attend(query_all, key_all, value_all):
    key_count, head_size = query_all.shape
    block_size = math.gcd(512, key_count)
    scaling = 1.0 / math.sqrt(head_size)

    def one_block(query_block):
        scores = jnp.dot(query_block, key_all.T, preferred_element_type=jnp.float32) * scaling
        weights = jax.nn.softmax(scores, axis=-1).astype(jnp.bfloat16)
        return jnp.dot(weights, value_all, preferred_element_type=jnp.float32).astype(jnp.bfloat16)

    blocks = query_all.reshape(key_count // block_size, block_size, head_size)
    return lax.map(one_block, blocks).reshape(key_count, head_size)


def body(
    stream_in, query_in, key_in, value_in, out_weight, norm_gain, up_weight, conv_taps, down_weight
):
    _, _, cols, dim = stream_in.shape
    views = lax.axis_size(VIEW)
    near = lax.axis_size(NEAR)
    spot = lax.axis_index(NEAR)
    heads = dim // HD
    hidden = up_weight.shape[1] // near

    mix_cols = dim // near
    mix_slice = lax.dynamic_slice_in_dim(out_weight, spot * mix_cols, mix_cols, 1)
    mix_part = lax.all_gather(mix_slice, VIEW, axis=0, tiled=True)
    mix_full = lax.all_gather(mix_part, NEAR, axis=0, tiled=False)
    up_slice = lax.dynamic_slice_in_dim(up_weight, spot * hidden, hidden, 1).T
    down_slice = lax.dynamic_slice_in_dim(down_weight, spot * hidden, hidden, 0)
    pair = lax.all_gather(jnp.stack([up_slice, down_slice]), VIEW, axis=1, tiled=True)
    up_rows, down_rows = pair[0], pair[1]
    taps_slice = lax.dynamic_slice_in_dim(conv_taps, spot * hidden, hidden, 2)
    taps = lax.all_gather(taps_slice, VIEW, axis=2, tiled=True)

    def split_heads(array):
        return array.reshape(cols, heads, HD).transpose(1, 0, 2)

    packed = jnp.stack([split_heads(a) for a in (query_in, key_in, value_in)], axis=1)
    moved = lax.all_to_all(packed, VIEW, split_axis=0, concat_axis=0, tiled=True)
    attended = attend(*(moved[:, i].reshape(views * cols, HD) for i in range(3)))
    back = lax.all_to_all(
        attended.reshape(views, cols, HD), VIEW, split_axis=0, concat_axis=0, tiled=True
    )
    tokens = back.transpose(1, 0, 2).reshape(cols, dim)

    mixed = jnp.einsum("tk,nkc->tnc", tokens, mix_full, preferred_element_type=jnp.float32)
    stream = stream_in.reshape(cols, dim).astype(jnp.float32) + mixed.reshape(cols, dim)
    normed = (
        stream * lax.rsqrt(jnp.mean(stream * stream, axis=-1, keepdims=True) + 1e-06) * norm_gain
    ).astype(jnp.bfloat16)

    piece = lax.all_gather(normed, NEAR, axis=0, tiled=True)
    up_proj = lax.dot_general(
        piece, up_rows, (((1,), (1,)), ((), ())), preferred_element_type=jnp.float32
    ).astype(jnp.bfloat16)
    units = up_rows.shape[0]
    image = up_proj.reshape(near, cols, units)
    low = lax.axis_index("zl") == 0
    edge = jnp.where(low, image[near - 1], image[0])
    other = lax.ppermute(edge, "zl", [(0, 1), (1, 0)])
    blank = jnp.zeros_like(other)
    rimmed = jnp.concatenate(
        [jnp.where(low, blank, other)[None], image, jnp.where(low, other, blank)[None]], axis=0
    )
    padded = jnp.pad(rimmed.astype(jnp.float32), ((0, 0), (1, 1), (0, 0)))
    conv_sum = jnp.zeros((near, cols, units), jnp.float32)
    for a in range(3):
        for b in range(3):
            conv_sum = conv_sum + taps[a, b] * padded[a : a + near, b : b + cols, :]
    activated = jax.nn.gelu(conv_sum).astype(jnp.bfloat16)
    product = jnp.dot(
        activated.reshape(-1, units), down_rows, preferred_element_type=jnp.float32
    ).astype(jnp.bfloat16)
    feed = lax.psum_scatter(product, NEAR, scatter_dimension=0, tiled=True)
    result = (stream + feed.astype(jnp.float32)).astype(jnp.bfloat16)
    return result.reshape(stream_in.shape)


def solution(mesh):
    fine = Mesh(mesh.devices.reshape(4, 4, 2, 4, 2), ("y", "zh", "zl", "x", "core"))
    tokens = P(VIEW, ROW, None, None)
    return jax.shard_map(
        body,
        mesh=fine,
        in_specs=(
            tokens,
            tokens,
            tokens,
            tokens,
            P(VIEW, None),
            P(),
            P(None, VIEW),
            P(None, None, VIEW),
            P(VIEW, None),
        ),
        out_specs=tokens,
        check_vma=False,
    )
```

time: 499 us -> 329 us (0.66)
  waiting for transfers between devices: 414 us -> 141 us
  blocking collectives: 0 us -> 86.5 us
  local copies, waits for them, and re-layouts: 6.7 us -> 37.6 us
  starting transfers between devices: 26.7 us -> 6.66 us
    reduce_scatter x2 -> x1, waiting for transfers between devices: 251 us -> 36.6 us  [body(): feed = lax.psum_scatter(product, NEAR, scatter_dimension=0, tiled=True)]
    all_gather x0 -> x1, blocking collectives: none -> 57.4 us  [body(): taps = lax.all_gather(taps_slice, VIEW, axis=2, tiled=True)]
    all_to_all x0 -> x1, blocking collectives: none -> 29.1 us  [body(): lax.all_to_all(attended.reshape(views, cols, HD), VIEW, split_axis=0, con...]
    all_gather x1 -> x4, waiting for transfers between devices: 103 us -> 76 us  [the longest x1 57.7 us: body(): mix_part = lax.all_gather(mix_slice, VIEW, axis=0, tiled=True)]
    all_to_all x3 -> x1, waiting for transfers between devices: 48.1 us -> 28.6 us  [body(): lax.all_to_all(packed, VIEW, split_axis=0, concat_axis=0, tiled=True)]
    slice x1 -> x2, local copies, waits for them, and re-layouts: 0.01 us -> 16.7 us  [the longest x1 15.5 us: body(): conv_sum = conv_sum + taps[a, b] * padded[a:a + near, b:b + cols, :]]
    all_to_all x3 -> x1, starting transfers between devices: 20.8 us -> 4.95 us  [body(): lax.all_to_all(packed, VIEW, split_axis=0, concat_axis=0, tiled=True)]
    ppermute x2 -> x1, waiting for transfers between devices: 11.5 us -> 0.01 us  [body(): other = lax.ppermute(edge, 'zl', [(0, 1), (1, 0)])]
  transfers between devices with their start and end apart: 8 -> 7, of which waited for: 8 -> 4; matrix products, arithmetic and copies ran while one was open for 1% -> 19% of each run, Pallas kernels for 0% -> 0%
where the time goes in v1:
time: 329 us; the launch traced here: 326 us
  waiting for transfers between devices  141 us (43%)
  blocking collectives  86.5 us (26%)
  local copies, waits for them, and re-layouts  37.6 us (11%)
  matrix products  29.6 us (9%)
  between operations  13.3 us (4%)
  other arithmetic  11.3 us (3%)
  starting transfers between devices  6.66 us (2%)
    all_gather x1, waiting for transfers between devices, body(): mix_part = lax.all_gather(mix_slice, VIEW, axis=0, tiled=True)  57.7 us
    all_gather x1, blocking collectives, body(): taps = lax.all_gather(taps_slice, VIEW, axis=2, tiled=True)  57.4 us
    reduce_scatter x1, waiting for transfers between devices, body(): feed = lax.psum_scatter(product, NEAR, scatter_dimension=0, tiled=True)  36.6 us
    all_to_all x1, blocking collectives, body(): lax.all_to_all(attended.reshape(views, cols, HD), VIEW, split_axis=0, con...  29.1 us
    all_to_all x1, waiting for transfers between devices, body(): lax.all_to_all(packed, VIEW, split_axis=0, concat_axis=0, tiled=True)  28.6 us
    all_gather x1, waiting for transfers between devices, body(): piece = lax.all_gather(normed, NEAR, axis=0, tiled=True)  18.2 us
    slice x1, local copies, waits for them, and re-layouts, body(): conv_sum = conv_sum + taps[a, b] * padded[a:a + near, b:b + cols, :]  15.5 us
    dot_general x1, local copies, waits for them, and re-layouts, body(): jnp.einsum('tk,nkc->tnc', tokens, mix_full, preferred_element_type=jnp.fl...  11.5 us
  transfers between devices with their start and end apart: 7, of which 4 were waited for; matrix products, arithmetic and copies ran while one was open for 19% of the time, Pallas kernels for 0%

profile of v1, /device:TPU:1, one launch (start us, length us, event | category | flops | bytes accessed | tf_op | source)
XLA Modules:
  0.0 326.3 jit_solution(4088880434286373642)
XLA Ops:
  6.6 1.6 constant_dynamic-slice_fusion.2
  8.3 57.7 %all-gather.6.cloned.1.call-done = bf16[2048,256]{1,0:T(8,128)(2,1)} async-done(((bf16[128,256]{1,0:T(8,128)(2,1)}), bf16[2048,256]{1,0:T(8,128)(2,1)}) %all-gather.6.cloned.1.call-update) | async-done | bytes 1048592 | tf_op jit(solution)/shard_map/all_gather | solution.py:40
  66.0 1.3 copy.29
  67.3 1.1 copy.27
  68.4 1.0 copy.28
  69.4 1.4 pad_maximum_fusion
  70.8 1.6 copy.30
  72.4 4.9 %all-to-all-start = ((bf16[16,3,128,128]{3,2,1,0:T(8,128)(2,1)}), bf16[16,3,128,128]{3,2,1,0:T(8,128)(2,1)S(1)}, u32[]{:S(2)}, u32[]{:S(2)}) async-start(bf16[16,3,128,128]{3,2,1,0:T(8,128)(2,1)} %copy.30), calls=%async_computation | async-start | bytes 3145728 | tf_op jit(solution)/shard_map/all_to_all | solution.py:53
  79.6 28.6 %all-to-all-done = bf16[16,3,128,128]{3,2,1,0:T(8,128)(2,1)S(1)} async-done(((bf16[16,3,128,128]{3,2,1,0:T(8,128)(2,1)}), bf16[16,3,128,128]{3,2,1,0:T(8,128)(2,1)S(1)}, u32[]{:S(2)}, u32[]{:S(2)}) %all-to-all-start) | async-done | bytes 1572896 | tf_op jit(solution)/shard_map/all_to_all | solution.py:53
  108.2 1.2 fusion.35
  109.4 17.6 %while.10 = (s32[]{:T(128)}, bf16[4,512,128]{2,1,0:T(8,128)(2,1)}, bf16[4,512,128]{2,1,0:T(8,128)(2,1)}, bf16[2048,128]{1,0:T(8,128)(2,1)S(1)}, bf16[2048,128]{1,0:T(8,128)(2,1)}, /*index=5*/s32[]{:T(128)}) while((s32[]{:T(128)}, bf16[4,512,128]{2,1,0:T(8,128)(2,1)}, bf16[4,512,128]{2,1,0:T(8,128)(2,1)}, bf16[2048,128]{1,0:T(8,128)(2,1)S(1)}, ...), condition=%wide.region_3.4_spmd, body=%wide.region_0.3_spmd.sunk | while | flops 546372608 | bytes 16002145 | solution.py:25
  109.4 1.7 multiply_reduce_fusion.3
  112.1 1.7 fusion.49
  113.8 1.7 multiply_reduce_fusion.3
  116.5 1.7 fusion.49
  118.2 1.7 multiply_reduce_fusion.3
  120.9 1.7 fusion.49
  122.6 1.7 multiply_reduce_fusion.3
  125.3 1.7 fusion.49
  127.0 29.1 %all_to_all.10 = bf16[16,128,128]{2,1,0:T(8,128)(2,1)S(1)} all-to-all(bf16[16,128,128]{2,1,0:T(8,128)(2,1)} %bitcast.83), channel_id=1, replica_groups=mesh['y'=4,'zh'=4,'zl'=2,'x'=4,'core'=2] {'y','zh'}, dimensions={0} | all-to-all | bytes 1048576 | tf_op jit(solution)/shard_map/all_to_all | solution.py:55
  156.4 11.5 %copy.32 = bf16[8,256,2048]{2,1,0:T(8,128)(2,1)} copy(bf16[8,256,2048]{1,2,0:T(8,128)(2,1)} %bitcast.74) | data formatting | bytes 16777216 | tf_op jit(solution)/shard_map/tk,nkc->tnc/dot_general | solution.py:60
  167.9 6.7 %multiply_reduce_fusion.1 = (f32[128]{0:T(128)S(1)}, f32[128,2048]{1,0:T(8,128)S(1)}) fusion(bf16[128,2048]{0,1:T(8,128)(2,1)S(1)} %bitcast.80, bf16[2048,2048]{1,0:T(8,128)(2,1)} %bitcast.72, bf16[1,1,128,2048]{3,2,1,0:T(8,128)(2,1)S(1)} %copy-done.4), kind=kOutput, calls=%fused_computation.55 | convolution fusion | flops 1074790272 | bytes 10486272 | tf_op jit(solution)/shard_map/tk,nkc->tnc/dot_general | solution.py:60
  174.6 1.0 multiply_convert_fusion
  175.8 57.4 %all_gather.21 = f32[3,3,512]{1,0,2:T(4,128)S(1)} all-gather(f32[3,3,32]{1,0,2:T(4,128)S(1)} %copy.35), channel_id=1, replica_groups=mesh['y'=4,'zh'=4,'zl'=2,'x'=4,'core'=2] {'y','zh'}, dimensions={2}, use_global_device_ids=true | all-gather | bytes 19584 | tf_op jit(solution)/shard_map/all_gather | solution.py:47
  233.3 18.2 %all-gather.8.cloned.1.call-done = bf16[1024,2048]{1,0:T(8,128)(2,1)} async-done(((bf16[128,2048]{1,0:T(8,128)(2,1)}), bf16[1024,2048]{1,0:T(8,128)(2,1)}) %all-gather.8.cloned.1.call-update) | async-done | bytes 4194320 | tf_op jit(solution)/shard_map/all_gather | solution.py:66
  251.5 5.2 %fusion.33 = bf16[1024,512]{1,0:T(8,128)(2,1)S(1)} fusion(bf16[1024,2048]{1,0:T(8,128)(2,1)} %all-gather.8.cloned.1.call-done, bf16[2,512,2048]{2,1,0:T(8,128)(2,1)} %all-gather.10.cloned.1.call-done), kind=kOutput, calls=%fused_computation.51 | convolution fusion | flops 2148007936 | bytes 7340032 | tf_op jit(solution)/shard_map/dot_general | solution.py:67
  256.8 1.5 collective-permute-start
  258.3 15.5 %slice_reduce_fusion.8 = (f32[512]{0:T(512)S(1)}, f32[512]{0:T(512)S(1)}, f32[512]{0:T(512)S(1)}, f32[512]{0:T(512)S(1)}, f32[512]{0:T(512)S(1)}, /*index=5*/f32...) fusion(f32[3,3,512]{1,0,2:T(4,128)S(1)} %all_gather.21), kind=kLoop, calls=%fused_computation.65 | loop fusion | bytes 36864 | tf_op jit(solution)/shard_map/slice | solution.py:83
  274.1 2.8 fusion.31
  276.9 4.3 %convolution_convert_fusion = bf16[1024,2048]{1,0:T(8,128)(2,1)} fusion(bf16[1024,512]{1,0:T(8,128)(2,1)S(1)} %bitcast.82, bf16[2,512,2048]{2,1,0:T(8,128)(2,1)S(1)} %copy-done.7), kind=kOutput, calls=%fused_computation.13 | convolution fusion | flops 2149580800 | bytes 7340032 | tf_op jit(solution)/shard_map/dot_general | solution.py:85
  281.2 36.6 %reduce-scatter.2.cloned.1.call-done = bf16[128,2048]{1,0:T(8,128)(2,1)} async-done(((bf16[1024,2048]{1,0:T(8,128)(2,1)}), bf16[128,2048]{1,0:T(8,128)(2,1)}) %reduce-scatter.2.cloned.1.call-update) | async-done | bytes 524304 | tf_op jit(solution)/shard_map/reduce_scatter | solution.py:88
  317.8 1.9 fusion.34
  (51 shorter events, 7.2 us)
Async XLA Ops:
  6.5 70.9 %copy-start = (bf16[2048,256]{1,0:T(8,128)(2,1)S(1)}, bf16[2048,256]{1,0:T(8,128)(2,1)}, u32[]{:S(2)}) copy-start(bf16[2048,256]{1,0:T(8,128)(2,1)} %param.17) | copy-start | bytes 3145732
  6.5 60.8 %copy-start.1 = (bf16[1,1,128,2048]{3,2,1,0:T(8,128)(2,1)S(1)}, bf16[1,1,128,2048]{3,2,1,0:T(8,128)(2,1)}, u32[]{:S(2)}) copy-start(bf16[1,1,128,2048]{3,2,1,0:T(8,128)(2,1)} %param.12) | copy-start | bytes 1572868
  6.5 61.8 %copy-start.2 = (bf16[1,1,128,2048]{3,2,1,0:T(8,128)(2,1)S(1)}, bf16[1,1,128,2048]{3,2,1,0:T(8,128)(2,1)}, u32[]{:S(2)}) copy-start(bf16[1,1,128,2048]{3,2,1,0:T(8,128)(2,1)} %param.13) | copy-start | bytes 1572868
  6.5 59.4 %all-gather.6.cloned.1.call-start = ((), (), s32[]{:S(2)}) async-start(), calls=%async_computation.3 | async-start | bytes 1114112 | tf_op jit(solution)/shard_map/all_gather | solution.py:40
  8.2 148.1 %all-gather.12.cloned.1.call-start = ((), (), s32[]{:S(2)}) async-start(), calls=%async_computation.7 | async-start | bytes 9437184 | tf_op jit(solution)/shard_map/all_gather | solution.py:41
  72.4 35.8 %all-to-all-start = ((bf16[16,3,128,128]{3,2,1,0:T(8,128)(2,1)}), bf16[16,3,128,128]{3,2,1,0:T(8,128)(2,1)S(1)}, u32[]{:S(2)}, u32[]{:S(2)}) async-start(bf16[16,3,128,128]{3,2,1,0:T(8,128)(2,1)} %copy.30), calls=%async_computation | async-start | bytes 3145728 | tf_op jit(solution)/shard_map/all_to_all | solution.py:53
  77.4 155.9 %all-gather.10.cloned.1.call-start = ((), (), s32[]{:S(2)}) async-start(), calls=%async_computation.5 | async-start | bytes 4456448 | tf_op jit(solution)/shard_map/all_gather | solution.py:44
  79.5 172.0 %all-gather.8.cloned.1.call-start = ((), (), s32[]{:S(2)}) async-start(), calls=%async_computation.4 | async-start | bytes 4718592 | tf_op jit(solution)/shard_map/all_gather | solution.py:66
  111.1 1.0 copy-start.3
  115.5 1.0 copy-start.3
  119.9 1.0 copy-start.3
  124.3 1.0 copy-start.3
  156.4 11.5 %copy-start.4 = (bf16[1,1,128,2048]{3,2,1,0:T(8,128)(2,1)S(1)}, bf16[1,1,128,2048]{3,2,1,0:T(8,128)(2,1)}, u32[]{:S(2)}) copy-start(bf16[1,1,128,2048]{3,2,1,0:T(8,128)(2,1)} %param.11) | copy-start | bytes 1572868
  167.9 6.7 %copy-start.5 = (f32[2048]{0:T(1024)S(1)}, f32[2048]{0:T(1024)}, u32[]{:S(2)}) copy-start(f32[2048]{0:T(1024)} %param.16) | copy-start | bytes 24580
  174.6 1.1 copy-start.6
  175.6 142.2 %reduce-scatter.2.cloned.1.call-start = ((), (), s32[]{:S(2)}) async-start(), calls=%async_computation.6 | async-start | bytes 4718592 | tf_op jit(solution)/shard_map/reduce_scatter | solution.py:88
  256.8 17.0 %collective-permute-start = (bf16[128,512]{1,0:T(8,128)(2,1)S(1)}, bf16[128,512]{1,0:T(8,128)(2,1)S(1)}, u32[]{:S(2)}, u32[]{:S(2)}) collective-permute-start(bf16[128,512]{1,0:T(8,128)(2,1)S(1)} %slice_select_fusion), channel_id=1, source_target_pairs={{0,8},{8,0},{1,9},{9,1},{2,10},{10,2},{3,11},{11,3},{4,12},{12,4},... | collective-permute-start | bytes 393224 | tf_op jit(solution)/shard_map/ppermute | solution.py:74
  274.1 2.8 copy-start.7
Sparse Core Ops, SparseCore 0:
  9.8 56.1 all-gather.5
  67.8 51.0 all-gather.11
  121.5 95.9 all-gather.9
  219.2 32.2 all-gather.7
  281.4 36.3 reduce-scatter.1

commit v2 on v1

v2 whole, which is shorter than its diff:
```python
import functools
import math

import jax
import jax.numpy as jnp
from jax import lax
from jax.experimental import pallas as pl
from jax.experimental.pallas import tpu as pltpu
from jax.sharding import Mesh, PartitionSpec as P

HD = 128
VIEW = ("y", "zh")
ROW = ("zl", "x", "core")
NEAR = ("x", "core")
F32 = jnp.float32
BF16 = jnp.bfloat16
BIG = 56 * 1024 * 1024


def cost(flops, bytes_accessed, transcendentals=0):
    return pl.CostEstimate(
        flops=int(flops), bytes_accessed=int(bytes_accessed), transcendentals=int(transcendentals)
    )


def pack_kernel(heads, cols, q_ref, k_ref, v_ref, taps_ref, out_ref, sems):
    copies = []
    for h in range(heads):
        for i, ref in enumerate((q_ref, k_ref, v_ref)):
            copies.append(
                pltpu.make_async_copy(
                    ref.at[:, pl.ds(h * HD, HD)],
                    out_ref.at[h, pl.ds(i * cols, cols), :],
                    sems.at[4 * h + i],
                )
            )
        copies.append(
            pltpu.make_async_copy(
                taps_ref, out_ref.at[h, pl.ds(3 * cols, taps_ref.shape[0]), :], sems.at[4 * h + 3]
            )
        )
    for copy in copies:
        copy.start()
    for copy in copies:
        copy.wait()


def pack(query, key, value, taps):
    cols, dim = query.shape
    heads = dim // HD
    hbm = pl.BlockSpec(memory_space=pl.ANY)
    return pl.pallas_call(
        functools.partial(pack_kernel, heads, cols),
        out_shape=jax.ShapeDtypeStruct((heads, 3 * cols + taps.shape[0], HD), BF16),
        in_specs=[hbm] * 4,
        out_specs=hbm,
        scratch_shapes=[pltpu.SemaphoreType.DMA((4 * heads,))],
        cost_estimate=cost(0, 4 * 3 * cols * dim),
        name="pack_heads",
    )(query, key, value, taps)


def attend_kernel(factor, spot_ref, q_ref, k_ref, v_ref, out_ref):
    views, cols, _ = q_ref.shape
    key = k_ref[...].reshape(-1, HD)
    value = v_ref[...].reshape(-1, HD)
    x_at, core_at = spot_ref[0], spot_ref[1]
    lane = lax.broadcasted_iota(jnp.int32, (cols, HD), 1)
    for i in range(views):
        scores = lax.dot_general(
            q_ref[i], key, (((1,), (1,)), ((), ())), preferred_element_type=F32
        )
        top = jnp.max(scores, axis=-1, keepdims=True)
        weights = jnp.exp2((scores - top) * factor)
        total = jnp.sum(weights, axis=-1, keepdims=True)
        mixed = jnp.dot(weights.astype(BF16), value, preferred_element_type=F32) / total
        mixed = pltpu.roll(mixed, lax.rem(HD - 32 * x_at, HD), 1)
        swapped = jnp.where(
            lane % 32 < 16, pltpu.roll(mixed, HD - 16, 1), pltpu.roll(mixed, 16, 1)
        )
        out_ref[i] = jnp.where(core_at == 0, mixed, swapped).astype(BF16)


def attend(moved, spot, cols, step_views=2):
    views = moved.shape[0]
    factor = math.log2(math.e) / math.sqrt(HD)
    tokens = views * cols
    return pl.pallas_call(
        functools.partial(attend_kernel, factor),
        out_shape=jax.ShapeDtypeStruct((views, cols, HD), BF16),
        grid_spec=pltpu.PrefetchScalarGridSpec(
            num_scalar_prefetch=1,
            grid=(views // step_views,),
            in_specs=[
                pl.BlockSpec((step_views, cols, HD), lambda i, s: (i, 0, 0)),
                pl.BlockSpec((views, cols, HD), lambda i, s: (0, 1, 0)),
                pl.BlockSpec((views, cols, HD), lambda i, s: (0, 2, 0)),
            ],
            out_specs=pl.BlockSpec((step_views, cols, HD), lambda i, s: (i, 0, 0)),
        ),
        compiler_params=pltpu.CompilerParams(vmem_limit_bytes=BIG),
        cost_estimate=cost(4 * tokens * tokens * HD, 8 * tokens * HD, tokens * tokens),
        name="attend",
    )(spot, moved, moved, moved)


def mix_kernel(back_ref, stream_ref, gain_ref, *refs):
    w_refs, stream_out, normed_out, acc = refs[:8], refs[8], refs[9], refs[10]
    step = pl.program_id(0)
    heads = back_ref.shape[0]

    @pl.when(step == 0)
    def _():
        acc[...] = stream_ref[...].astype(F32)

    left = jnp.concatenate([back_ref[h] for h in range(heads)], axis=1)
    right = jnp.concatenate([w[h] for h in range(heads) for w in w_refs], axis=0)
    acc[...] += jnp.dot(left, right, preferred_element_type=F32)

    @pl.when(step == pl.num_programs(0) - 1)
    def _():
        stream = acc[...]
        stream_out[...] = stream
        scale = lax.rsqrt(jnp.mean(stream * stream, axis=-1, keepdims=True) + 1e-06)
        normed_out[...] = (stream * scale * gain_ref[...]).astype(BF16)


def mix(back, stream_in, gain, pieces, step_heads=2):
    heads, cols, _ = back.shape
    dim = stream_in.shape[1]
    strip = pieces[0].shape[1]
    whole = pl.BlockSpec((cols, dim), lambda i: (0, 0))
    return pl.pallas_call(
        mix_kernel,
        out_shape=[
            jax.ShapeDtypeStruct((cols, dim), F32),
            jax.ShapeDtypeStruct((cols, dim), BF16),
        ],
        grid=(heads // step_heads,),
        in_specs=[
            pl.BlockSpec((step_heads, cols, HD), lambda i: (i, 0, 0)),
            whole,
            pl.BlockSpec((1, dim), lambda i: (0, 0)),
        ]
        + [pl.BlockSpec((step_heads, strip, dim), lambda i: (i, 0, 0))] * len(pieces),
        out_specs=[whole, whole],
        scratch_shapes=[pltpu.VMEM((cols, dim), F32)],
        compiler_params=pltpu.CompilerParams(vmem_limit_bytes=BIG),
        cost_estimate=cost(2 * cols * dim * dim, 2 * dim * dim + 8 * cols * dim),
        name="mix_norm",
    )(back, stream_in, gain.reshape(1, dim), *pieces)


def up_kernel(x_ref, w_ref, out_ref):
    weight = w_ref[...].reshape(-1, w_ref.shape[-1])
    out_ref[0] = lax.dot_general(
        x_ref[0], weight, (((1,), (1,)), ((), ())), preferred_element_type=F32
    ).astype(BF16)


def up(piece, pair):
    rows, cols, dim = piece.shape
    views, both, _ = pair.shape
    units = views * both // 2
    return pl.pallas_call(
        up_kernel,
        out_shape=jax.ShapeDtypeStruct((rows, cols, units), BF16),
        grid=(rows,),
        in_specs=[
            pl.BlockSpec((1, cols, dim), lambda i: (i, 0, 0)),
            pl.BlockSpec((views, both // 2, dim), lambda i: (0, 0, 0)),
        ],
        out_specs=pl.BlockSpec((1, cols, units), lambda i: (i, 0, 0)),
        compiler_params=pltpu.CompilerParams(vmem_limit_bytes=BIG),
        cost_estimate=cost(2 * rows * cols * dim * units, 2 * dim * (rows * cols + units)),
        name="up",
    )(piece, pair)


def conv_kernel(low_ref, above_ref, row_ref, below_ref, other_ref, taps_ref, w_ref, out_ref):
    step, last = pl.program_id(0), pl.num_programs(0) - 1
    low = low_ref[0]
    cols, units = row_ref.shape[1:]
    keep_above = jnp.where((step > 0) | (low == 0), 1.0, 0.0)
    keep_below = jnp.where((step < last) | (low == 1), 1.0, 0.0)
    col = lax.broadcasted_iota(jnp.int32, (cols, HD), 0)
    parts = []
    for u in range(0, units, HD):
        at = pl.ds(u, HD)
        other = other_ref[:, at].astype(F32)
        above = jnp.where(step == 0, other, above_ref[0, :, at].astype(F32)) * keep_above
        below = jnp.where(step == last, other, below_ref[0, :, at].astype(F32)) * keep_below
        row = row_ref[0, :, at].astype(F32)
        sums = []
        for b in range(3):
            sums.append(
                taps_ref[pl.ds(b, 1), at] * above
                + taps_ref[pl.ds(3 + b, 1), at] * row
                + taps_ref[pl.ds(6 + b, 1), at] * below
            )
        conv = (
            sums[1]
            + jnp.where(col == 0, 0.0, pltpu.roll(sums[0], 1, 0))
            + jnp.where(col == cols - 1, 0.0, pltpu.roll(sums[2], cols - 1, 0))
        )
        inner = math.sqrt(2.0 / math.pi) * (conv + 0.044715 * (conv * conv * conv))
        parts.append((0.5 * conv * (1.0 + jnp.tanh(inner))).astype(BF16))
    active = jnp.concatenate(parts, axis=1)
    weight = w_ref[...].reshape(-1, w_ref.shape[-1])
    out_ref[0] = jnp.dot(active, weight, preferred_element_type=F32).astype(BF16)


def conv_down(low, hidden, other, taps, pair):
    rows, cols, units = hidden.shape
    views, both, dim = pair.shape
    row = functools.partial(pl.BlockSpec, (1, cols, units))
    return pl.pallas_call(
        conv_kernel,
        out_shape=jax.ShapeDtypeStruct((rows, cols, dim), BF16),
        grid_spec=pltpu.PrefetchScalarGridSpec(
            num_scalar_prefetch=1,
            grid=(rows,),
            in_specs=[
                row(lambda i, s: (jnp.maximum(i - 1, 0), 0, 0)),
                row(lambda i, s: (i, 0, 0)),
                row(lambda i, s: (jnp.minimum(i + 1, rows - 1), 0, 0)),
                pl.BlockSpec((cols, units), lambda i, s: (0, 0)),
                pl.BlockSpec(taps.shape, lambda i, s: (0, 0)),
                pl.BlockSpec((views, both // 2, dim), lambda i, s: (0, 1, 0)),
            ],
            out_specs=pl.BlockSpec((1, cols, dim), lambda i, s: (i, 0, 0)),
        ),
        compiler_params=pltpu.CompilerParams(vmem_limit_bytes=BIG),
        cost_estimate=cost(2 * rows * cols * dim * units, 2 * dim * (rows * cols + units)),
        name="conv_gelu_down",
    )(low, hidden, hidden, hidden, other, taps, pair)


def shift(array, axis, by):
    count = lax.axis_size(axis)
    return lax.ppermute(array, axis, [(i, (i + by) % count) for i in range(count)])


def body(
    stream_in, query_in, key_in, value_in, out_weight, norm_gain, up_weight, conv_taps, down_weight
):
    shape = stream_in.shape
    _, _, cols, dim = shape
    views = lax.axis_size(VIEW)
    near = lax.axis_size(NEAR)
    spot = lax.axis_index(NEAR)
    x_at, core_at = lax.axis_index("x"), lax.axis_index("core")
    part = up_weight.shape[1] // near
    flat = [a.reshape(cols, dim) for a in (stream_in, query_in, key_in, value_in)]

    own_taps = lax.dynamic_slice_in_dim(conv_taps, spot * part, part, 2).reshape(-1)
    high = lax.reduce_precision(own_taps, 8, 7)
    middle = lax.reduce_precision(own_taps - high, 8, 7)
    terms = jnp.concatenate([high, middle, own_taps - high - middle])
    term_rows = 8 * pl.cdiv(terms.size, 8 * HD)
    terms = jnp.pad(terms, (0, term_rows * HD - terms.size)).astype(BF16).reshape(term_rows, HD)

    packed = pack(*flat[1:], terms)
    moved = lax.all_to_all(packed, VIEW, split_axis=0, concat_axis=0, tiled=True)
    attended = attend(moved, jnp.stack([x_at, core_at]).astype(jnp.int32), cols)
    back = lax.all_to_all(attended, VIEW, split_axis=0, concat_axis=0, tiled=True)

    strip = out_weight.shape[0] // near
    mine = lax.dynamic_slice_in_dim(out_weight, spot * strip, strip, 0)
    mine = lax.all_gather(mine, VIEW, axis=0, tiled=False)
    up_slice = lax.dynamic_slice_in_dim(up_weight, spot * part, part, 1).T
    down_slice = lax.dynamic_slice_in_dim(down_weight, spot * part, part, 0)
    pair, mine = lax.optimization_barrier((jnp.concatenate([up_slice, down_slice]), mine))
    pair = lax.all_gather(pair, VIEW, axis=0, tiled=False)
    before, after = shift(mine, "x", 1), shift(mine, "x", -1)
    half = views // 2
    across = jnp.concatenate([shift(before[:half], "x", 1), shift(after[half:], "x", -1)])
    pieces = []
    for piece in (mine, after, across, before):
        pieces += [piece, shift(piece, "core", 1)]

    stream, normed = mix(back, flat[0], norm_gain, pieces)

    taps = moved[:, 3 * cols :].reshape(views, -1)[:, : 27 * part].astype(F32)
    taps = jnp.sum(taps.reshape(views, 3, 9, part), axis=1)
    taps = taps.transpose(1, 0, 2).reshape(9, views * part)
    piece = lax.all_gather(normed, NEAR, axis=0, tiled=False)
    hidden = up(piece, pair)
    low = lax.axis_index("zl")
    edge = jnp.where(low == 0, hidden[near - 1], hidden[0])
    other = shift(edge, "zl", 1)
    product = conv_down((1 - low).astype(jnp.int32).reshape(1), hidden, other, taps, pair)
    feed = lax.psum_scatter(product.reshape(-1, dim), NEAR, scatter_dimension=0, tiled=True)
    return (stream + feed.astype(F32)).astype(BF16).reshape(shape)


def solution(mesh):
    fine = Mesh(mesh.devices.reshape(4, 4, 2, 4, 2), ("y", "zh", "zl", "x", "core"))
    tokens = P(VIEW, ROW, None, None)
    return jax.shard_map(
        body,
        mesh=fine,
        in_specs=(
            tokens,
            tokens,
            tokens,
            tokens,
            P(VIEW, None),
            P(),
            P(None, VIEW),
            P(None, None, VIEW),
            P(VIEW, None),
        ),
        out_specs=tokens,
        check_vma=False,
    )
```

time: 329 us -> 333 us (1.012)
  Pallas kernels: 0 us -> 92.6 us
  blocking collectives: 86.5 us -> 0 us
  waiting for transfers between devices: 141 us -> 187 us
  local copies, waits for them, and re-layouts: 37.6 us -> 7.78 us
  matrix products: 29.6 us -> 0 us
  starting transfers between devices: 6.66 us -> 24.7 us
  other arithmetic: 11.3 us -> 5.03 us
    pallas_call x0 -> x5, Pallas kernels: none -> 92.6 us  [the longest x1 50.3 us: pack(): pl.pallas_call(functools.partial(pack_kernel, heads, cols), out_shape=jax...]
    all_gather x1 -> x0, blocking collectives: 57.4 us -> none  [body(): taps = lax.all_gather(taps_slice, VIEW, axis=2, tiled=True)]
    dot_general x11 -> x0, matrix products: 29.6 us -> none  [the longest x4 6.76 us: one_block(): jnp.dot(query_block, key_all.T, preferred_element_type=jnp.float32)]
    all_to_all x1 -> x0, blocking collectives: 29.1 us -> none  [body(): lax.all_to_all(attended.reshape(views, cols, HD), VIEW, split_axis=0, con...]
    ppermute x1 -> x9, waiting for transfers between devices: 0.01 us -> 27.4 us  [shift(): lax.ppermute(array, axis, [(i, (i + by) % count) for i in range(count)])]
    slice x2 -> x3, local copies, waits for them, and re-layouts: 16.7 us -> 0.84 us  [the longest x1 0.76 us: body(): taps = moved[:, 3 * cols:].reshape(views, -1)[:, :27 * part].astype(F32)]
    all_to_all x0 -> x1, waiting for transfers between devices: none -> 15.2 us  [body(): lax.all_to_all(attended, VIEW, split_axis=0, concat_axis=0, tiled=True)]
    ppermute x1 -> x9, starting transfers between devices: 1.54 us -> 15.3 us  [shift(): lax.ppermute(array, axis, [(i, (i + by) % count) for i in range(count)])]
  transfers between devices with their start and end apart: 7 -> 15, of which waited for: 4 -> 8; matrix products, arithmetic and copies ran while one was open for 19% -> 2% of each run, Pallas kernels for 0% -> 22%
where the time goes in v2:
time: 333 us; the launch traced here: 330 us
  waiting for transfers between devices  187 us (56%)
  Pallas kernels  92.6 us (28%)
  starting transfers between devices  24.7 us (7%)
  between operations  13.3 us (4%)
  local copies, waits for them, and re-layouts  7.78 us (2%)
  other arithmetic  5.03 us (2%)
    all_gather x1, waiting for transfers between devices, body(): mine = lax.all_gather(mine, VIEW, axis=0, tiled=False)  55.7 us
    pallas_call x1, Pallas kernels, pack(): pl.pallas_call(functools.partial(pack_kernel, heads, cols), out_shape=jax...  50.3 us
    reduce_scatter x1, waiting for transfers between devices, body(): lax.psum_scatter(product.reshape(-1, dim), NEAR, scatter_dimension=0, til...  38 us
    all_gather x1, waiting for transfers between devices, body(): piece = lax.all_gather(normed, NEAR, axis=0, tiled=False)  33.5 us
    ppermute x9, waiting for transfers between devices, shift(): lax.ppermute(array, axis, [(i, (i + by) % count) for i in range(count)])  27.4 us
    all_to_all x1, waiting for transfers between devices, body(): lax.all_to_all(packed, VIEW, split_axis=0, concat_axis=0, tiled=True)  16.8 us
    ppermute x9, starting transfers between devices, shift(): lax.ppermute(array, axis, [(i, (i + by) % count) for i in range(count)])  15.3 us
    all_to_all x1, waiting for transfers between devices, body(): lax.all_to_all(attended, VIEW, split_axis=0, concat_axis=0, tiled=True)  15.2 us
  transfers between devices with their start and end apart: 15, of which 8 were waited for; matrix products, arithmetic and copies ran while one was open for 2% of the time, Pallas kernels for 22%

profile of v2, /device:TPU:1, one launch (start us, length us, event | category | flops | bytes accessed | tf_op | source)
XLA Modules:
  0.0 330.0 jit_solution(11986631913849338450)
XLA Ops:
  6.5 1.6 constant_dynamic-slice_fusion
  8.6 0.9 constant_dynamic-slice_fusion.1
  9.5 0.7 pad_maximum_fusion
  10.3 55.7 %all-gather.7.cloned.1.call-done = bf16[256,2048]{1,0:T(8,128)(2,1)} async-done(((bf16[16,2048]{1,0:T(8,128)(2,1)}), bf16[256,2048]{1,0:T(8,128)(2,1)}) %all-gather.7.cloned.1.call-update) | async-done | bytes 1048592 | tf_op jit(solution)/shard_map/all_gather | solution.py:270
  66.0 0.8 constant_dynamic-slice_fusion.3
  66.9 0.7 fusion.8.taps_ref
  67.5 50.3 %pack_heads.1 = bf16[16,392,128]{2,1,0:T(8,128)(2,1)} custom-call(bf16[128,2048]{1,0:T(8,128)(2,1)} %bitcast.30, bf16[128,2048]{1,0:T(8,128)(2,1)} %bitcast.31, bf16[128,2048]{1,0:T(8,128)(2,1)} %bitcast.32, bf16[8,128]{1,0:T(8,128)(2,1)} %fusion.8.taps_ref), custom_call_target="tpu_custom_call" | custom-call | bytes 3145728 | tf_op jit(solution)/shard_map/pack_heads/pallas_call | solution.py:52
  117.8 5.0 %all-to-all-start = ((bf16[16,392,128]{2,1,0:T(8,128)(2,1)}), bf16[16,392,128]{2,1,0:T(8,128)(2,1)}, u32[]{:S(2)}, u32[]{:S(2)}) async-start(bf16[16,392,128]{2,1,0:T(8,128)(2,1)} %pack_heads.1), calls=%async_computation | async-start | bytes 3211264 | tf_op jit(solution)/shard_map/all_to_all | solution.py:264
  122.9 1.3 collective-permute-start.3
  124.1 1.5 collective-permute-start.1
  125.6 21.1 %collective-permute-done.3.refs_6_ = bf16[16,16,2048]{2,1,0:T(8,128)(2,1)S(1)} collective-permute-done((bf16[16,16,2048]{2,1,0:T(8,128)(2,1)}, bf16[16,16,2048]{2,1,0:T(8,128)(2,1)S(1)}, u32[]{:S(2)}, u32[]{:S(2)}) %collective-permute-start.3) | collective-permute-done | bytes 1048608 | tf_op jit(solution)/shard_map/ppermute | solution.py:241
  146.9 2.7 collective-permute-start.5
  150.3 3.8 %collective-permute-start = (bf16[16,16,2048]{2,1,0:T(8,128)(2,1)}, bf16[16,16,2048]{2,1,0:T(8,128)(2,1)}, u32[]{:S(2)}, u32[]{:S(2)}) collective-permute-start(bf16[16,16,2048]{2,1,0:T(8,128)(2,1)} %bitcast.9.refs_0_), channel_id=1, source_target_pairs={{0,1},{1,0},{2,3},{3,2},{4,5},{5,4},{6,7},{7,6},{8,9},{9,8},{10,11... | collective-permute-start | bytes 3145736 | tf_op jit(solution)/shard_map/ppermute | solution.py:241
  154.6 3.7 %collective-permute-done.4 = bf16[8,16,2048]{2,1,0:T(8,128)(2,1)S(1)} collective-permute-done((bf16[8,16,2048]{2,1,0:T(8,128)(2,1)S(1)}, bf16[8,16,2048]{2,1,0:T(8,128)(2,1)S(1)}, u32[]{:S(2)}, u32[]{:S(2)}) %collective-permute-start.4) | collective-permute-done | bytes 524320 | tf_op jit(solution)/shard_map/ppermute | solution.py:241
  158.3 0.8 constant_dynamic-update-slice_fusion.1
  159.1 0.8 constant_dynamic-update-slice_fusion.refs_4_
  160.0 4.1 %collective-permute-start.6 = (bf16[16,16,2048]{2,1,0:T(8,128)(2,1)}, bf16[16,16,2048]{2,1,0:T(8,128)(2,1)}, u32[]{:S(2)}, u32[]{:S(2)}) collective-permute-start(bf16[16,16,2048]{2,1,0:T(8,128)(2,1)} %constant_dynamic-update-slice_fusion.refs_4_), channel_id=1, source_target_pairs={{0,1},{1,0},{2,3},{3,2},{4,5},{5,4},{6,7},{7,6},{8,9},{9,8},{10,11... | collective-permute-start | bytes 3145736 | tf_op jit(solution)/shard_map/ppermute | solution.py:241
  164.0 16.8 %all-to-all-done.q_ref.k_ref.v_ref = bf16[16,392,128]{2,1,0:T(8,128)(2,1)} async-done(((bf16[16,392,128]{2,1,0:T(8,128)(2,1)}), bf16[16,392,128]{2,1,0:T(8,128)(2,1)}, u32[]{:S(2)}, u32[]{:S(2)}) %all-to-all-start) | async-done | bytes 1605664 | tf_op jit(solution)/shard_map/all_to_all | solution.py:264
  180.8 13.4 %attend.1 = bf16[16,128,128]{2,1,0:T(8,128)(2,1)} custom-call(s32[2]{0:T(128)} %pad_add_fusion.spot_ref, bf16[16,392,128]{2,1,0:T(8,128)(2,1)} %all-to-all-done.q_ref.k_ref.v_ref, bf16[16,392,128]{2,1,0:T(8,128)(2,1)} %all-to-all-done.q_ref.k_ref.v_ref, bf16[16,392,128]{2,1,0:T(8,128)(2,1)} %all-to-all-done.q_ref.k_ref.v_ref), custom_call_target="tpu_custom_call" | custom-call | flops 2147483648 | bytes 2097152 | tf_op jit(solution)/shard_map/attend/pallas_call | solution.py:88
  194.2 4.2 %all-to-all-start.1 = ((bf16[16,128,128]{2,1,0:T(8,128)(2,1)}), bf16[16,128,128]{2,1,0:T(8,128)(2,1)}, u32[]{:S(2)}, u32[]{:S(2)}) async-start(bf16[16,128,128]{2,1,0:T(8,128)(2,1)} %attend.1), calls=%async_computation.1 | async-start | bytes 1048576 | tf_op jit(solution)/shard_map/all_to_all | solution.py:266
  198.5 15.2 %all-to-all-done.1.back_ref = bf16[16,128,128]{2,1,0:T(8,128)(2,1)} async-done(((bf16[16,128,128]{2,1,0:T(8,128)(2,1)}), bf16[16,128,128]{2,1,0:T(8,128)(2,1)}, u32[]{:S(2)}, u32[]{:S(2)}) %all-to-all-start.1) | async-done | bytes 524320 | tf_op jit(solution)/shard_map/all_to_all | solution.py:266
  213.7 8.7 %mix_norm.1 = (f32[128,2048]{1,0:T(8,128)}, bf16[128,2048]{1,0:T(8,128)(2,1)}) custom-call(bf16[16,128,128]{2,1,0:T(8,128)(2,1)} %all-to-all-done.1.back_ref, bf16[128,2048]{1,0:T(8,128)(2,1)} %bitcast.33, f32[1,2048]{1,0:T(1,128)} %bitcast.36, bf16[16,16,2048]{2,1,0:T(8,128)(2,1)} %bitcast.9.refs_0_, bf16[16,16,2048]{2,1,0:T(8,128)(2,1)} %collective-permute-done.refs_1_, ...), custom_call_target="tpu_custom_call" | custom-call | flops 1073741824 | bytes 10485760 | tf_op jit(solution)/shard_map/mix_norm/pallas_call | solution.py:133
  222.5 0.8 slice.28
  223.3 33.5 %all-gather.9.cloned.1.call-done = bf16[1024,2048]{1,0:T(8,128)(2,1)} async-done(((bf16[128,2048]{1,0:T(8,128)(2,1)}), bf16[1024,2048]{1,0:T(8,128)(2,1)}) %all-gather.9.cloned.1.call-update) | async-done | bytes 4194320 | tf_op jit(solution)/shard_map/all_gather | solution.py:287
  256.8 10.0 %up.1.above_ref.row_ref.below_ref = bf16[8,128,512]{2,1,0:T(8,128)(2,1)} custom-call(bf16[8,128,2048]{2,1,0:T(8,128)(2,1)} %bitcast.27, bf16[16,64,2048]{2,1,0:T(8,128)(2,1)} %bitcast.24), custom_call_target="tpu_custom_call" | custom-call | flops 2147483648 | bytes 6291456 | tf_op jit(solution)/shard_map/up/pallas_call | solution.py:165
  266.9 1.0 fusion.1
  267.9 1.4 collective-permute-start.8
  269.5 0.7 reshape.55.taps_ref
  270.2 2.7 collective-permute-done.8.other_ref
  273.5 10.1 %conv_gelu_down.1 = bf16[8,128,2048]{2,1,0:T(8,128)(2,1)} custom-call(s32[1]{0:T(128)} %bitcast.10.low_ref, bf16[8,128,512]{2,1,0:T(8,128)(2,1)} %up.1.above_ref.row_ref.below_ref, bf16[8,128,512]{2,1,0:T(8,128)(2,1)} %up.1.above_ref.row_ref.below_ref, bf16[8,128,512]{2,1,0:T(8,128)(2,1)} %up.1.above_ref.row_ref.below_ref, bf16[128,512]{1,0:T(8,128)(2,1)} %copy-done.4, ...), custom_call_target="tpu_custom_call" | custom-call | flops 2147483648 | bytes 6291456 | tf_op jit(solution)/shard_map/conv_gelu_down/pallas_call | solution.py:217
  283.6 38.0 %reduce-scatter.2.cloned.1.call-done = bf16[128,2048]{1,0:T(8,128)(2,1)} async-done(((bf16[1024,2048]{1,0:T(8,128)(2,1)}), bf16[128,2048]{1,0:T(8,128)(2,1)}) %reduce-scatter.2.cloned.1.call-update) | async-done | bytes 524304 | tf_op jit(solution)/shard_map/reduce_scatter | solution.py:293
  321.6 1.9 fusion
  (40 shorter events, 2.9 us)
Async XLA Ops:
  6.5 1.6 copy-start
  6.5 59.4 %all-gather.7.cloned.1.call-start = ((), (), s32[]{:S(2)}) async-start(), calls=%async_computation.4 | async-start | bytes 1114112 | tf_op jit(solution)/shard_map/all_gather | solution.py:270
  8.1 215.2 %all-gather.11.cloned.1.call-start = ((), (), s32[]{:S(2)}) async-start(), calls=%async_computation.6 | async-start | bytes 4456448 | tf_op jit(solution)/shard_map/all_gather | solution.py:274
  117.8 62.9 %all-to-all-start = ((bf16[16,392,128]{2,1,0:T(8,128)(2,1)}), bf16[16,392,128]{2,1,0:T(8,128)(2,1)}, u32[]{:S(2)}, u32[]{:S(2)}) async-start(bf16[16,392,128]{2,1,0:T(8,128)(2,1)} %pack_heads.1), calls=%async_computation | async-start | bytes 3211264 | tf_op jit(solution)/shard_map/all_to_all | solution.py:264
  122.9 23.8 %collective-permute-start.3 = (bf16[16,16,2048]{2,1,0:T(8,128)(2,1)}, bf16[16,16,2048]{2,1,0:T(8,128)(2,1)S(1)}, u32[]{:S(2)}, u32[]{:S(2)}) collective-permute-start(bf16[16,16,2048]{2,1,0:T(8,128)(2,1)} %bitcast.9.refs_0_), channel_id=1, source_target_pairs={{0,2},{2,4},{4,6},{6,0},{1,3},{3,5},{5,7},{7,1},{8,10},{10,12},{12... | collective-permute-start | bytes 3145736 | tf_op jit(solution)/shard_map/ppermute | solution.py:241
  124.1 22.7 %collective-permute-start.1 = (bf16[16,16,2048]{2,1,0:T(8,128)(2,1)}, bf16[16,16,2048]{2,1,0:T(8,128)(2,1)S(1)}, u32[]{:S(2)}, u32[]{:S(2)}) collective-permute-start(bf16[16,16,2048]{2,1,0:T(8,128)(2,1)} %bitcast.9.refs_0_), channel_id=1, source_target_pairs={{0,6},{2,0},{4,2},{6,4},{1,7},{3,1},{5,3},{7,5},{8,14},{10,8},{12,... | collective-permute-start | bytes 3145736 | tf_op jit(solution)/shard_map/ppermute | solution.py:241
  146.7 47.5 %copy-start.1 = (bf16[16,16,2048]{2,1,0:T(8,128)(2,1)}, bf16[16,16,2048]{2,1,0:T(8,128)(2,1)S(1)}, u32[]{:S(2)}) copy-start(bf16[16,16,2048]{2,1,0:T(8,128)(2,1)S(1)} %collective-permute-done.3.refs_6_) | copy-start | bytes 3145732
  146.7 11.6 %collective-permute-start.4 = (bf16[8,16,2048]{2,1,0:T(8,128)(2,1)S(1)}, bf16[8,16,2048]{2,1,0:T(8,128)(2,1)S(1)}, u32[]{:S(2)}, u32[]{:S(2)}) collective-permute-start(bf16[8,16,2048]{2,1,0:T(8,128)(2,1)S(1)} %slice.24), channel_id=1, source_target_pairs={{0,2},{2,4},{4,6},{6,0},{1,3},{3,5},{5,7},{7,1},{8,10},{10,12},{12... | collective-permute-start | bytes 1572872 | tf_op jit(solution)/shard_map/ppermute | solution.py:241
  146.8 47.4 %copy-start.2 = (bf16[16,16,2048]{2,1,0:T(8,128)(2,1)}, bf16[16,16,2048]{2,1,0:T(8,128)(2,1)S(1)}, u32[]{:S(2)}) copy-start(bf16[16,16,2048]{2,1,0:T(8,128)(2,1)S(1)} %collective-permute-done.1.refs_2_) | copy-start | bytes 3145732
  146.9 12.2 %collective-permute-start.5 = (bf16[8,16,2048]{2,1,0:T(8,128)(2,1)S(1)}, bf16[8,16,2048]{2,1,0:T(8,128)(2,1)S(1)}, u32[]{:S(2)}, u32[]{:S(2)}) collective-permute-start(bf16[8,16,2048]{2,1,0:T(8,128)(2,1)S(1)} %slice.25), channel_id=1, source_target_pairs={{0,6},{2,0},{4,2},{6,4},{1,7},{3,1},{5,3},{7,5},{8,14},{10,8},{12,... | collective-permute-start | bytes 1572872 | tf_op jit(solution)/shard_map/ppermute | solution.py:241
  150.3 48.3 %collective-permute-start = (bf16[16,16,2048]{2,1,0:T(8,128)(2,1)}, bf16[16,16,2048]{2,1,0:T(8,128)(2,1)}, u32[]{:S(2)}, u32[]{:S(2)}) collective-permute-start(bf16[16,16,2048]{2,1,0:T(8,128)(2,1)} %bitcast.9.refs_0_), channel_id=1, source_target_pairs={{0,1},{1,0},{2,3},{3,2},{4,5},{5,4},{6,7},{7,6},{8,9},{9,8},{10,11... | collective-permute-start | bytes 3145736 | tf_op jit(solution)/shard_map/ppermute | solution.py:241
  154.1 59.6 %collective-permute-start.2 = (bf16[16,16,2048]{2,1,0:T(8,128)(2,1)S(1)}, bf16[16,16,2048]{2,1,0:T(8,128)(2,1)}, u32[]{:S(2)}, u32[]{:S(2)}) collective-permute-start(bf16[16,16,2048]{2,1,0:T(8,128)(2,1)S(1)} %collective-permute-done.1.refs_2_), channel_id=1, source_target_pairs={{0,1},{1,0},{2,3},{3,2},{4,5},{5,4},{6,7},{7,6},{8,9},{9,8},{10,11... | collective-permute-start | bytes 3145736 | tf_op jit(solution)/shard_map/ppermute | solution.py:241
  154.1 59.6 %collective-permute-start.7 = (bf16[16,16,2048]{2,1,0:T(8,128)(2,1)S(1)}, bf16[16,16,2048]{2,1,0:T(8,128)(2,1)}, u32[]{:S(2)}, u32[]{:S(2)}) collective-permute-start(bf16[16,16,2048]{2,1,0:T(8,128)(2,1)S(1)} %collective-permute-done.3.refs_6_), channel_id=1, source_target_pairs={{0,1},{1,0},{2,3},{3,2},{4,5},{5,4},{6,7},{7,6},{8,9},{9,8},{10,11... | collective-permute-start | bytes 3145736 | tf_op jit(solution)/shard_map/ppermute | solution.py:241
  160.0 53.8 %collective-permute-start.6 = (bf16[16,16,2048]{2,1,0:T(8,128)(2,1)}, bf16[16,16,2048]{2,1,0:T(8,128)(2,1)}, u32[]{:S(2)}, u32[]{:S(2)}) collective-permute-start(bf16[16,16,2048]{2,1,0:T(8,128)(2,1)} %constant_dynamic-update-slice_fusion.refs_4_), channel_id=1, source_target_pairs={{0,1},{1,0},{2,3},{3,2},{4,5},{5,4},{6,7},{7,6},{8,9},{9,8},{10,11... | collective-permute-start | bytes 3145736 | tf_op jit(solution)/shard_map/ppermute | solution.py:241
  194.2 19.5 %all-to-all-start.1 = ((bf16[16,128,128]{2,1,0:T(8,128)(2,1)}), bf16[16,128,128]{2,1,0:T(8,128)(2,1)}, u32[]{:S(2)}, u32[]{:S(2)}) async-start(bf16[16,128,128]{2,1,0:T(8,128)(2,1)} %attend.1), calls=%async_computation.1 | async-start | bytes 1048576 | tf_op jit(solution)/shard_map/all_to_all | solution.py:266
  198.5 58.4 %all-gather.9.cloned.1.call-start = ((), (), s32[]{:S(2)}) async-start(), calls=%async_computation.5 | async-start | bytes 4718592 | tf_op jit(solution)/shard_map/all_gather | solution.py:287
  222.5 99.1 %reduce-scatter.2.cloned.1.call-start = ((), (), s32[]{:S(2)}) async-start(), calls=%async_computation.3 | async-start | bytes 4718592 | tf_op jit(solution)/shard_map/reduce_scatter | solution.py:293
  267.9 4.9 %collective-permute-start.8 = (bf16[128,512]{1,0:T(8,128)(2,1)S(1)}, bf16[128,512]{1,0:T(8,128)(2,1)S(1)}, u32[]{:S(2)}, u32[]{:S(2)}) collective-permute-start(bf16[128,512]{1,0:T(8,128)(2,1)S(1)} %fusion.1), channel_id=1, source_target_pairs={{0,8},{8,0},{1,9},{9,1},{2,10},{10,2},{3,11},{11,3},{4,12},{12,4},... | collective-permute-start | bytes 393224 | tf_op jit(solution)/shard_map/ppermute | solution.py:241
  272.8 0.7 copy-start.4
  283.6 38.0 %copy-start.3 = (f32[128,2048]{1,0:T(8,128)S(1)}, f32[128,2048]{1,0:T(8,128)}, u32[]{:S(2)}) copy-start(f32[128,2048]{1,0:T(8,128)} %get-tuple-element.10) | copy-start | bytes 3145732
Sparse Core Ops, SparseCore 0:
  9.8 56.1 all-gather.6
  68.4 92.5 all-gather.10
  222.6 34.2 all-gather.8
  283.7 37.7 reduce-scatter.1

commit v3 on v1

v3 whole, which is shorter than its diff:
```python
import functools
import math

import jax
import jax.numpy as jnp
from jax import lax
from jax.experimental import pallas as pl
from jax.experimental.pallas import tpu as pltpu
from jax.sharding import Mesh, PartitionSpec as P

HD = 128
VIEW = ("y", "zh")
ROW = ("zl", "x", "core")
NEAR = ("x", "core")
F32 = jnp.float32
BF16 = jnp.bfloat16
MIB = 1024 * 1024
VMEM = pl.BlockSpec(memory_space=pltpu.VMEM)
SMEM = pl.BlockSpec(memory_space=pltpu.SMEM)


def call(kernel, name, limit, out_shape, in_specs, args, hides=False, out_specs=None, scratch=()):
    return pl.pallas_call(
        kernel,
        out_shape=out_shape,
        in_specs=in_specs,
        out_specs=out_specs or jax.tree.map(lambda _: VMEM, out_shape),
        scratch_shapes=list(scratch),
        compiler_params=pltpu.CompilerParams(vmem_limit_bytes=limit * MIB),
        cost_estimate=pl.CostEstimate(
            flops=30_000_000_000 if hides else 1000, bytes_accessed=1000, transcendentals=0
        ),
        name=name,
    )(*args)


def pack_kernel(q_ref, k_ref, v_ref, out_ref):
    heads, cols = out_ref.shape[0], q_ref.shape[0]
    for h in range(heads):
        for i, ref in enumerate((q_ref, k_ref, v_ref)):
            out_ref[h, pl.ds(i * cols, cols), :] = ref[:, pl.ds(h * HD, HD)]


def pack(query, key, value):
    cols, dim = query.shape
    shape = jax.ShapeDtypeStruct((dim // HD, 3 * cols, HD), BF16)
    return call(pack_kernel, "pack_heads", 6, shape, [VMEM] * 3, (query, key, value))


def attend_kernel(factor, step, moved_ref, out_ref):
    views, cols, _ = out_ref.shape
    key = moved_ref[:, pl.ds(cols, cols), :].reshape(-1, HD)
    value = moved_ref[:, pl.ds(2 * cols, cols), :].reshape(-1, HD)
    for i in range(0, views, step):
        query = moved_ref[pl.ds(i, step), pl.ds(0, cols), :].reshape(-1, HD)
        scores = lax.dot_general(
            query, key, (((1,), (1,)), ((), ())), preferred_element_type=F32
        )
        top = jnp.max(scores, axis=-1, keepdims=True)
        weights = jnp.exp2((scores - top) * factor)
        total = jnp.sum(weights, axis=-1, keepdims=True)
        mixed = jnp.dot(weights.astype(BF16), value, preferred_element_type=F32) / total
        out_ref[pl.ds(i, step)] = mixed.astype(BF16).reshape(step, cols, HD)


def attend(moved, cols):
    factor = math.log2(math.e) / math.sqrt(HD)
    shape = jax.ShapeDtypeStruct((moved.shape[0], cols, HD), BF16)
    return call(
        functools.partial(attend_kernel, factor, 2), "attend", 24, shape, [VMEM], (moved,), True
    )


def join_kernel(back_ref, out_ref):
    for h in range(back_ref.shape[0]):
        out_ref[:, pl.ds(h * HD, HD)] = back_ref[h]


def join(back):
    heads, cols, size = back.shape
    shape = jax.ShapeDtypeStruct((cols, heads * size), BF16)
    return call(join_kernel, "join_heads", 4, shape, [VMEM], (back,), True)


def mix_kernel(spot_ref, left_ref, stream_ref, gain_ref, *refs):
    w_refs, (stream_out, normed_out, acc, sem) = refs[:-4], refs[-4:]
    width = w_refs[0].shape[2]
    left = left_ref[...]
    for i, w_ref in enumerate(w_refs):
        core_at = spot_ref[1] if i % 2 == 0 else 1 - spot_ref[1]
        block = 2 * lax.rem(spot_ref[0] + i // 2, 4) + core_at
        at = pl.ds(pl.multiple_of(block * width, width), width)
        weight = w_ref[...].reshape(-1, width)
        acc[:, at] = stream_ref[:, at].astype(F32) + jnp.dot(
            left, weight, preferred_element_type=F32
        )
    copy = pltpu.make_async_copy(acc, stream_out, sem)
    copy.start()
    stream = acc[...]
    scale = lax.rsqrt(jnp.mean(stream * stream, axis=-1, keepdims=True) + 1e-06)
    normed_out[...] = (stream * scale * gain_ref[...]).astype(BF16)
    copy.wait()


def mix(spot, left, stream_in, gain, pieces):
    shapes = [jax.ShapeDtypeStruct(stream_in.shape, t) for t in (F32, BF16)]
    args = (spot, left, stream_in, gain.reshape(1, -1), *pieces)
    return call(
        mix_kernel,
        "mix_norm",
        8,
        shapes,
        [SMEM] + [VMEM] * (len(args) - 1),
        args,
        out_specs=[pl.BlockSpec(memory_space=pl.ANY), VMEM],
        scratch=[pltpu.VMEM(stream_in.shape, F32), pltpu.SemaphoreType.DMA],
    )


def up_kernel(spot_ref, *refs):
    rows_refs, (w_ref, out_ref, edge_ref) = refs[:-3], refs[-3:]
    first, low = spot_ref[1] == 0, spot_ref[4]
    rows = []
    for same_ref, other_ref in zip(rows_refs[::2], rows_refs[1::2]):
        same, other = same_ref[...], other_ref[...]
        rows += [jnp.where(first, same, other), jnp.where(first, other, same)]
    out = lax.dot_general(
        jnp.concatenate(rows), w_ref[...], (((1,), (1,)), ((), ())), preferred_element_type=F32
    )
    out_ref[...] = out.astype(BF16).reshape(out_ref.shape)
    edge_ref[...] = out_ref[2 * lax.rem(4 - low - spot_ref[0], 4) + low]


def up(spot, rows, weight):
    cols, units = rows[0].shape[0], weight.shape[0]
    shapes = [
        jax.ShapeDtypeStruct((len(rows), cols, units), BF16),
        jax.ShapeDtypeStruct((cols, units), BF16),
    ]
    args = (spot, *rows, weight)
    return call(up_kernel, "up", 16, shapes, [SMEM] + [VMEM] * (len(args) - 1), args)


def conv_kernel(offsets, spot_ref, *refs):
    hidden_ref, edge_ref, taps_ref, w_ref, *outs = refs
    cols, units = edge_ref.shape
    core_at, low = spot_ref[1], spot_ref[4]
    col = lax.broadcasted_iota(jnp.int32, (cols, HD), 0)
    for n, offset in enumerate(offsets):
        x_at = lax.rem(spot_ref[0] + offset, 4)
        first_x, last_x = x_at == 0, x_at == 3
        keep_above = jnp.where(first_x & (low == 1), 0.0, 1.0)
        keep_below = jnp.where(last_x & (low == 0), 0.0, 1.0)
        places = (2 * offset - 1) % 8, 2 * offset, 2 * offset + 1, (2 * offset + 2) % 8
        parts = [[], []]
        for u in range(0, units, HD):
            at = pl.ds(u, HD)
            edge = edge_ref[:, at].astype(F32)
            rows = [hidden_ref[place, :, at].astype(F32) for place in places]
            rows[0] = jnp.where(first_x, edge, rows[0]) * keep_above
            rows[3] = jnp.where(last_x, edge, rows[3]) * keep_below
            for r in range(2):
                sums = [
                    taps_ref[pl.ds(b, 1), at] * rows[r]
                    + taps_ref[pl.ds(3 + b, 1), at] * rows[r + 1]
                    + taps_ref[pl.ds(6 + b, 1), at] * rows[r + 2]
                    for b in range(3)
                ]
                conv = (
                    sums[1]
                    + jnp.where(col == 0, 0.0, pltpu.roll(sums[0], 1, 0))
                    + jnp.where(col == cols - 1, 0.0, pltpu.roll(sums[2], cols - 1, 0))
                )
                inner = math.sqrt(2.0 / math.pi) * (conv + 0.044715 * (conv * conv * conv))
                parts[r].append((0.5 * conv * (1.0 + jnp.tanh(inner))).astype(BF16))
        active = jnp.concatenate([jnp.concatenate(p, axis=1) for p in parts], axis=0)
        out = jnp.dot(active, w_ref[...], preferred_element_type=F32)
        top, bottom = out[:cols].astype(BF16), out[cols:].astype(BF16)
        outs[2 * n][...] = jnp.where(core_at == 0, bottom, top)
        outs[2 * n + 1][...] = jnp.where(core_at == 0, top, bottom)


def conv_down(spot, offsets, hidden, edge, taps, weight, hides):
    cols = edge.shape[0]
    shape = jax.ShapeDtypeStruct((cols, weight.shape[1]), BF16)
    args = (spot, hidden, edge, taps, weight)
    return call(
        functools.partial(conv_kernel, offsets),
        "conv_gelu_down",
        14,
        [shape] * (2 * len(offsets)),
        [SMEM] + [VMEM] * (len(args) - 1),
        args,
        hides,
    )


def shift(array, axis, by):
    count = lax.axis_size(axis)
    return lax.ppermute(array, axis, [(i, (i + by) % count) for i in range(count)])


def after_all(array, *others):
    return lax.optimization_barrier((array, *others))[0]


def body(
    stream_in, query_in, key_in, value_in, out_weight, norm_gain, up_weight, conv_taps, down_weight
):
    shape = stream_in.shape
    _, _, cols, dim = shape
    views = lax.axis_size(VIEW)
    near = lax.axis_size(NEAR)
    at = lax.axis_index(NEAR)
    part = up_weight.shape[1] // near
    low = 1 - lax.axis_index("zl")
    spot = jnp.stack(
        [lax.axis_index(name) for name in ("x", "core", "y", "zh")] + [low]
    ).astype(jnp.int32)
    flat = [a.reshape(cols, dim) for a in (stream_in, query_in, key_in, value_in)]

    width = dim // near
    mine = lax.dynamic_slice_in_dim(out_weight, at * width, width, 1)
    mine = lax.all_gather(mine, VIEW, axis=0, tiled=False)

    packed = pack(*flat[1:])
    moved = lax.all_to_all(packed, VIEW, split_axis=0, concat_axis=0, tiled=True)
    attended = attend(moved, cols)
    back = lax.all_to_all(attended, VIEW, split_axis=0, concat_axis=0, tiled=True)

    own_taps = lax.dynamic_slice_in_dim(conv_taps, at * part, part, 2).reshape(-1)
    high = lax.reduce_precision(own_taps, 8, 7)
    middle = lax.reduce_precision(own_taps - high, 8, 7)
    terms = jnp.concatenate([high, middle, own_taps - high - middle])
    terms = jnp.pad(terms, (0, 8 * dim - terms.size)).astype(BF16).reshape(8, dim)
    up_slice = lax.dynamic_slice_in_dim(up_weight, at * part, part, 1).T
    down_slice = lax.dynamic_slice_in_dim(down_weight, at * part, part, 0)
    pair = after_all(jnp.concatenate([up_slice, down_slice, terms]), mine)
    pair = lax.all_gather(pair, VIEW, axis=0, tiled=False)

    half = views // 2
    mine = after_all(mine, moved[0, :8])
    before, after = shift(mine, "x", 1), shift(mine, "x", -1)
    across = jnp.concatenate([shift(before[:half], "x", 1), shift(after[half:], "x", -1)])
    pieces = []
    for piece in (mine, after, across, before):
        pieces += [piece, shift(piece, "core", 1)]
    stream, normed = mix(spot, join(back), flat[0], norm_gain, pieces)

    up_rows = pair[:, :part].reshape(-1, dim)
    down_rows = pair[:, part : 2 * part].reshape(-1, dim)
    taps = pair[:, 2 * part :].reshape(views, -1)[:, : 27 * part].astype(F32)
    taps = jnp.sum(taps.reshape(views, 3, 9, part), axis=1)
    taps = taps.transpose(1, 0, 2).reshape(9, views * part)

    half = cols // 2
    before, after = shift(normed, "x", 1), shift(normed, "x", -1)
    across = jnp.concatenate([shift(before[:half], "x", 1), shift(after[half:], "x", -1)])
    rows = []
    for row in (normed, after, across, before):
        rows += [row, shift(row, "core", 1)]
    hidden, edge = up(spot, rows, up_rows)
    edge = shift(edge, "zl", 1)

    def add(*terms):
        return sum(term.astype(F32) for term in terms).astype(BF16)

    give, keep_2 = conv_down(spot, (2,), hidden, edge, taps, down_rows, False)
    got_2 = shift(give, "core", 1)
    give_1, keep_1, give_3, keep_3, give_0, keep_0 = conv_down(
        spot, (1, 3, 0), hidden, edge, taps, down_rows, True
    )
    got_1, got_3, got_0 = (shift(give, "core", 1) for give in (give_1, give_3, give_0))
    total = add(keep_2, got_2)
    right, left = shift(total[:half], "x", 1), shift(total[half:], "x", -1)
    blank = jnp.zeros_like(left)
    right = add(keep_1, got_1, jnp.concatenate([right, blank]))
    left = add(keep_3, got_3, jnp.concatenate([blank, left]))
    right, left = shift(right, "x", 1), shift(left, "x", -1)
    result = stream
    for term in (keep_0, got_0, right, left):
        result = result + term.astype(F32)
    return result.astype(BF16).reshape(shape)


def solution(mesh):
    fine = Mesh(mesh.devices.reshape(4, 4, 2, 4, 2), ("y", "zh", "zl", "x", "core"))
    tokens = P(VIEW, ROW, None, None)
    return jax.shard_map(
        body,
        mesh=fine,
        in_specs=(
            tokens,
            tokens,
            tokens,
            tokens,
            P(VIEW, None),
            P(),
            P(None, VIEW),
            P(None, None, VIEW),
            P(VIEW, None),
        ),
        out_specs=tokens,
        check_vma=False,
    )
```

time: 329 us -> 224 us (0.68)
  blocking collectives: 86.5 us -> 0 us
  starting transfers between devices: 6.66 us -> 49.3 us
  waiting for transfers between devices: 141 us -> 103 us
  matrix products: 29.6 us -> 0 us
  Pallas kernels: 0 us -> 26 us
  local copies, waits for them, and re-layouts: 37.6 us -> 25.6 us
  other arithmetic: 11.3 us -> 3.57 us
    all_gather x1 -> x0, blocking collectives: 57.4 us -> none  [body(): taps = lax.all_gather(taps_slice, VIEW, axis=2, tiled=True)]
    ppermute x1 -> x25, waiting for transfers between devices: 0.01 us -> 42.9 us  [shift(): lax.ppermute(array, axis, [(i, (i + by) % count) for i in range(count)])]
    reduce_scatter x1 -> x0, waiting for transfers between devices: 36.6 us -> none  [body(): feed = lax.psum_scatter(product, NEAR, scatter_dimension=0, tiled=True)]
    dot_general x11 -> x0, matrix products: 29.6 us -> none  [the longest x4 6.76 us: one_block(): jnp.dot(query_block, key_all.T, preferred_element_type=jnp.float32)]
    ppermute x1 -> x25, starting transfers between devices: 1.54 us -> 30.9 us  [shift(): lax.ppermute(array, axis, [(i, (i + by) % count) for i in range(count)])]
    all_to_all x1 -> x0, blocking collectives: 29.1 us -> none  [body(): lax.all_to_all(attended.reshape(views, cols, HD), VIEW, split_axis=0, con...]
    all_to_all x1, waiting for transfers between devices: 28.6 us -> 0.01 us  [body(): lax.all_to_all(packed, VIEW, split_axis=0, concat_axis=0, tiled=True)]
    pallas_call x0 -> x7, Pallas kernels: none -> 26 us  [call(): pl.pallas_call(kernel, out_shape=out_shape, in_specs=in_specs, out_specs=...]
  transfers between devices with their start and end apart: 7 -> 29, of which waited for: 4 -> 10; matrix products, arithmetic and copies ran while one was open for 19% -> 9% of each run, Pallas kernels for 0% -> 9%
where the time goes in v3:
time: 224 us; the launch traced here: 221 us
  waiting for transfers between devices  103 us (46%)
  starting transfers between devices  49.3 us (22%)
  Pallas kernels  26 us (12%)
  local copies, waits for them, and re-layouts  25.6 us (11%)
  between operations  13.8 us (6%)
  other arithmetic  3.57 us (2%)
    all_gather x1, waiting for transfers between devices, body(): mine = lax.all_gather(mine, VIEW, axis=0, tiled=False)  48.9 us
    ppermute x25, waiting for transfers between devices, shift(): lax.ppermute(array, axis, [(i, (i + by) % count) for i in range(count)])  42.9 us
    ppermute x25, starting transfers between devices, shift(): lax.ppermute(array, axis, [(i, (i + by) % count) for i in range(count)])  30.9 us
    pallas_call x7, Pallas kernels, call(): pl.pallas_call(kernel, out_shape=out_shape, in_specs=in_specs, out_specs=...  26 us
    all_to_all x1, starting transfers between devices, body(): lax.all_to_all(packed, VIEW, split_axis=0, concat_axis=0, tiled=True)  11.9 us
    all_gather x1, waiting for transfers between devices, body(): pair = lax.all_gather(pair, VIEW, axis=0, tiled=False)  10.8 us
    unnamed x30, local copies, waits for them, and re-layouts  10.2 us
    all_to_all x1, starting transfers between devices, body(): lax.all_to_all(attended, VIEW, split_axis=0, concat_axis=0, tiled=True)  6.52 us
  transfers between devices with their start and end apart: 29, of which 10 were waited for; matrix products, arithmetic and copies ran while one was open for 9% of the time, Pallas kernels for 9%

profile of v3, /device:TPU:1, one launch (start us, length us, event | category | flops | bytes accessed | tf_op | source)
XLA Modules:
  0.0 221.0 jit_solution(4314536942766886353)
XLA Ops:
  6.5 1.6 constant_dynamic-slice_fusion.3
  11.3 1.5 pack_heads.1
  12.7 11.9 %all-to-all-start = ((bf16[16,384,128]{2,1,0:T(8,128)(2,1)}), bf16[16,384,128]{2,1,0:T(8,128)(2,1)}, u32[]{:S(2)}, u32[]{:S(2)}) async-start(bf16[16,384,128]{2,1,0:T(8,128)(2,1)} %pack_heads.1), calls=%async_computation | async-start | bytes 3145728 | tf_op jit(solution)/shard_map/all_to_all | solution.py:227
  27.1 48.9 %all-gather.5.cloned.1.call-done = bf16[2048,256]{1,0:T(8,128)(2,1)} async-done(((bf16[128,256]{1,0:T(8,128)(2,1)}), bf16[2048,256]{1,0:T(8,128)(2,1)}) %all-gather.5.cloned.1.call-update) | async-done | bytes 1048592 | tf_op jit(solution)/shard_map/all_gather | solution.py:224
  76.1 1.4 collective-permute-start.3
  77.5 1.4 collective-permute-start.1
  79.0 7.6 %attend.1 = bf16[16,128,128]{2,1,0:T(8,128)(2,1)S(1)} custom-call(bf16[16,384,128]{2,1,0:T(8,128)(2,1)} %all-to-all-done.moved_ref), custom_call_target="tpu_custom_call" | custom-call | flops 30000001024 | bytes 1000 | tf_op jit(solution)/shard_map/attend/pallas_call | solution.py:23
  87.4 6.5 %all-to-all-start.1 = ((bf16[16,128,128]{2,1,0:T(8,128)(2,1)}), bf16[16,128,128]{2,1,0:T(8,128)(2,1)}, u32[]{:S(2)}, u32[]{:S(2)}) async-start(bf16[16,128,128]{2,1,0:T(8,128)(2,1)} %copy-done.7), calls=%async_computation.1 | async-start | bytes 1048576 | tf_op jit(solution)/shard_map/all_to_all | solution.py:229
  94.0 6.6 %collective-permute-done.3.refs_6_ = bf16[16,128,256]{2,1,0:T(8,128)(2,1)S(1)} collective-permute-done((bf16[16,128,256]{2,1,0:T(8,128)(2,1)}, bf16[16,128,256]{2,1,0:T(8,128)(2,1)S(1)}, u32[]{:S(2)}, u32[]{:S(2)}) %collective-permute-start.3) | collective-permute-done | bytes 1048608 | tf_op jit(solution)/shard_map/ppermute | solution.py:200
  102.5 2.5 %collective-permute-start.5 = (bf16[8,128,256]{2,1,0:T(8,128)(2,1)}, bf16[8,128,256]{2,1,0:T(8,128)(2,1)}, u32[]{:S(2)}, u32[]{:S(2)}) collective-permute-start(bf16[8,128,256]{2,1,0:T(8,128)(2,1)} %slice.42), channel_id=1, source_target_pairs={{0,6},{2,0},{4,2},{6,4},{1,7},{3,1},{5,3},{7,5},{8,14},{10,8},{12,... | collective-permute-start | bytes 1572872 | tf_op jit(solution)/shard_map/ppermute | solution.py:200
  105.0 3.2 %collective-permute-start = (bf16[16,128,256]{2,1,0:T(8,128)(2,1)}, bf16[16,128,256]{2,1,0:T(8,128)(2,1)}, u32[]{:S(2)}, u32[]{:S(2)}) collective-permute-start(bf16[16,128,256]{2,1,0:T(8,128)(2,1)} %bitcast.25), channel_id=1, source_target_pairs={{0,1},{1,0},{2,3},{3,2},{4,5},{5,4},{6,7},{7,6},{8,9},{9,8},{10,11... | collective-permute-start | bytes 3145736 | tf_op jit(solution)/shard_map/ppermute | solution.py:200
  108.8 5.0 %collective-permute-done.4 = bf16[8,128,256]{2,1,0:T(8,128)(2,1)} collective-permute-done((bf16[8,128,256]{2,1,0:T(8,128)(2,1)}, bf16[8,128,256]{2,1,0:T(8,128)(2,1)}, u32[]{:S(2)}, u32[]{:S(2)}) %collective-permute-start.4) | collective-permute-done | bytes 524320 | tf_op jit(solution)/shard_map/ppermute | solution.py:200
  113.7 1.9 constant_dynamic-update-slice_fusion.1
  115.6 1.9 constant_dynamic-update-slice_fusion.refs_4_
  117.5 3.5 %collective-permute-start.6 = (bf16[16,128,256]{2,1,0:T(8,128)(2,1)}, bf16[16,128,256]{2,1,0:T(8,128)(2,1)}, u32[]{:S(2)}, u32[]{:S(2)}) collective-permute-start(bf16[16,128,256]{2,1,0:T(8,128)(2,1)} %constant_dynamic-update-slice_fusion.refs_4_), channel_id=1, source_target_pairs={{0,1},{1,0},{2,3},{3,2},{4,5},{5,4},{6,7},{7,6},{8,9},{9,8},{10,11... | collective-permute-start | bytes 3145736 | tf_op jit(solution)/shard_map/ppermute | solution.py:200
  123.7 5.3 %mix_norm.1 = (f32[128,2048]{1,0:T(8,128)S(1)}, bf16[128,2048]{1,0:T(8,128)(2,1)}) custom-call(s32[5]{0:T(128)S(1)} %stack.23.spot_ref, bf16[128,2048]{1,0:T(8,128)(2,1)S(1)} %join_heads.1.left_ref, bf16[128,2048]{1,0:T(8,128)(2,1)S(1)} %bitcast.27, f32[1,2048]{1,0:T(1,128)S(1)} %bitcast.31, bf16[16,128,256]{2,1,0:T(8,128)(2,1)S(1)} %bitcast.26, ...), custom_call_target="tpu_custom_call" | custom-call | flops 1000 | bytes 1000 | tf_op jit(solution)/shard_map/mix_norm/pallas_call | solution.py:23
  130.0 2.7 %collective-permute-start.9 = (bf16[128,2048]{1,0:T(8,128)(2,1)}, bf16[128,2048]{1,0:T(8,128)(2,1)}, u32[]{:S(2)}, u32[]{:S(2)}) collective-permute-start(bf16[128,2048]{1,0:T(8,128)(2,1)} %get-tuple-element.19.refs_0_), channel_id=1, source_target_pairs={{0,6},{2,0},{4,2},{6,4},{1,7},{3,1},{5,3},{7,5},{8,14},{10,8},{12,... | collective-permute-start | bytes 1572872 | tf_op jit(solution)/shard_map/ppermute | solution.py:200
  132.6 12.2 %collective-permute-done.11.refs_6_ = bf16[128,2048]{1,0:T(8,128)(2,1)} collective-permute-done((bf16[128,2048]{1,0:T(8,128)(2,1)}, bf16[128,2048]{1,0:T(8,128)(2,1)}, u32[]{:S(2)}, u32[]{:S(2)}) %collective-permute-start.11) | collective-permute-done | bytes 524320 | tf_op jit(solution)/shard_map/ppermute | solution.py:200
  146.9 2.7 %collective-permute-start.13 = (bf16[64,2048]{1,0:T(8,128)(2,1)S(1)}, bf16[64,2048]{1,0:T(8,128)(2,1)S(1)}, u32[]{:S(2)}, u32[]{:S(2)}) collective-permute-start(bf16[64,2048]{1,0:T(8,128)(2,1)S(1)} %slice.44), channel_id=1, source_target_pairs={{0,6},{2,0},{4,2},{6,4},{1,7},{3,1},{5,3},{7,5},{8,14},{10,8},{12,... | collective-permute-start | bytes 786440 | tf_op jit(solution)/shard_map/ppermute | solution.py:200
  149.6 1.6 collective-permute-start.8
  151.7 2.3 %collective-permute-done.12 = bf16[64,2048]{1,0:T(8,128)(2,1)S(1)} collective-permute-done((bf16[64,2048]{1,0:T(8,128)(2,1)S(1)}, bf16[64,2048]{1,0:T(8,128)(2,1)S(1)}, u32[]{:S(2)}, u32[]{:S(2)}) %collective-permute-start.12) | collective-permute-done | bytes 262176 | tf_op jit(solution)/shard_map/ppermute | solution.py:200
  155.5 1.8 collective-permute-start.14
  157.3 10.8 %all-gather.7.cloned.1.call-done = bf16[1152,2048]{1,0:T(8,128)(2,1)} async-done(((bf16[72,2048]{1,0:T(8,128)(2,1)}), bf16[1152,2048]{1,0:T(8,128)(2,1)}) %all-gather.7.cloned.1.call-update) | async-done | bytes 4718608 | tf_op jit(solution)/shard_map/all_gather | solution.py:239
  169.2 2.6 %fusion.7 = (bf16[16,32,2048]{2,1,0:T(8,128)(2,1)S(1)}, bf16[16,32,2048]{2,1,0:T(8,128)(2,1)S(1)}) fusion(bf16[16,72,2048]{2,1,0:T(8,128)(2,1)} %bitcast.33), kind=kLoop, calls=%fused_computation.26 | loop fusion | bytes 8388608 | tf_op jit(solution)/shard_map/slice | solution.py:251
  171.8 4.6 %up.1 = (bf16[8,128,512]{2,1,0:T(8,128)(2,1)S(1)}, bf16[128,512]{1,0:T(8,128)(2,1)S(1)}) custom-call(s32[5]{0:T(128)S(1)} %stack.23.spot_ref, bf16[128,2048]{1,0:T(8,128)(2,1)} %get-tuple-element.19.refs_0_, bf16[128,2048]{1,0:T(8,128)(2,1)} %collective-permute-done.8.refs_1_, bf16[128,2048]{1,0:T(8,128)(2,1)} %collective-permute-done.9.refs_2_, ...), custom_call_target="tpu_custom_call" | custom-call | flops 1000 | bytes 1000 | tf_op jit(solution)/shard_map/up/pallas_call | solution.py:23
  183.0 1.8 conv_gelu_down.3
  184.8 1.6 collective-permute-start.19
  186.4 4.0 %conv_gelu_down.2 = (bf16[128,2048]{1,0:T(8,128)(2,1)S(1)}, bf16[128,2048]{1,0:T(8,128)(2,1)S(1)}, bf16[128,2048]{1,0:T(8,128)(2,1)S(1)}, bf16[128,2048]{1,0:T(8...) custom-call(s32[5]{0:T(128)S(1)} %stack.23.spot_ref, bf16[8,128,512]{2,1,0:T(8,128)(2,1)S(1)} %copy-done.4, ...), custom_call_target="tpu_custom_call" | custom-call | flops 30000001024 | bytes 1000 | tf_op jit(solution)/shard_map/conv_gelu_down/pallas_call | solution.py:23
  192.7 1.5 collective-permute-start.23
  194.3 5.1 %collective-permute-done.20 = bf16[64,2048]{1,0:T(8,128)(2,1)S(1)} collective-permute-done((bf16[64,2048]{1,0:T(8,128)(2,1)S(1)}, bf16[64,2048]{1,0:T(8,128)(2,1)S(1)}, u32[]{:S(2)}, u32[]{:S(2)}) %collective-permute-start.20) | collective-permute-done | bytes 262176 | tf_op jit(solution)/shard_map/ppermute | solution.py:200
  200.3 2.8 %collective-permute-start.24 = (bf16[128,2048]{1,0:T(8,128)(2,1)S(1)}, bf16[128,2048]{1,0:T(8,128)(2,1)S(1)}, u32[]{:S(2)}, u32[]{:S(2)}) collective-permute-start(bf16[128,2048]{1,0:T(8,128)(2,1)S(1)} %add_convert_fusion.1), channel_id=1, source_target_pairs={{0,6},{2,0},{4,2},{6,4},{1,7},{3,1},{5,3},{7,5},{8,14},{10,8},{12,... | collective-permute-start | bytes 1572872 | tf_op jit(solution)/shard_map/ppermute | solution.py:200
  203.1 9.9 %collective-permute-done.21 = bf16[128,2048]{1,0:T(8,128)(2,1)S(1)} collective-permute-done((bf16[128,2048]{1,0:T(8,128)(2,1)S(1)}, bf16[128,2048]{1,0:T(8,128)(2,1)S(1)}, u32[]{:S(2)}, u32[]{:S(2)}) %collective-permute-start.21) | collective-permute-done | bytes 524320 | tf_op jit(solution)/shard_map/ppermute | solution.py:200
  (93 shorter events, 28.4 us)
Async XLA Ops:
  6.5 18.5 %copy-start = (bf16[2048,256]{1,0:T(8,128)(2,1)S(1)}, bf16[2048,256]{1,0:T(8,128)(2,1)}, u32[]{:S(2)}) copy-start(bf16[2048,256]{1,0:T(8,128)(2,1)} %param.15) | copy-start | bytes 3145732
  6.5 69.5 %all-gather.5.cloned.1.call-start = ((), (), s32[]{:S(2)}) async-start(), calls=%async_computation.2 | async-start | bytes 1114112 | tf_op jit(solution)/shard_map/all_gather | solution.py:224
  12.7 12.0 %copy-start.12 = (f32[3,3,256]{2,1,0:T(4,128)S(1)}, f32[3,3,256]{2,1,0:T(4,128)}, u32[]{:S(2)}) copy-start(f32[3,3,256]{2,1,0:T(4,128)} %param.16) | copy-start | bytes 27652
  12.7 66.3 %all-to-all-start = ((bf16[16,384,128]{2,1,0:T(8,128)(2,1)}), bf16[16,384,128]{2,1,0:T(8,128)(2,1)}, u32[]{:S(2)}, u32[]{:S(2)}) async-start(bf16[16,384,128]{2,1,0:T(8,128)(2,1)} %pack_heads.1), calls=%async_computation | async-start | bytes 3145728 | tf_op jit(solution)/shard_map/all_to_all | solution.py:227
  24.7 143.4 %all-gather.7.cloned.1.call-start = ((), (), s32[]{:S(2)}) async-start(), calls=%async_computation.3 | async-start | bytes 5013504 | tf_op jit(solution)/shard_map/all_gather | solution.py:239
  76.1 24.5 %collective-permute-start.3 = (bf16[16,128,256]{2,1,0:T(8,128)(2,1)}, bf16[16,128,256]{2,1,0:T(8,128)(2,1)S(1)}, u32[]{:S(2)}, u32[]{:S(2)}) collective-permute-start(bf16[16,128,256]{2,1,0:T(8,128)(2,1)} %bitcast.23), channel_id=1, source_target_pairs={{0,2},{2,4},{4,6},{6,0},{1,3},{3,5},{5,7},{7,1},{8,10},{10,12},{12... | collective-permute-start | bytes 3145736 | tf_op jit(solution)/shard_map/ppermute | solution.py:200
  77.5 24.1 %collective-permute-start.1 = (bf16[16,128,256]{2,1,0:T(8,128)(2,1)}, bf16[16,128,256]{2,1,0:T(8,128)(2,1)S(1)}, u32[]{:S(2)}, u32[]{:S(2)}) collective-permute-start(bf16[16,128,256]{2,1,0:T(8,128)(2,1)} %bitcast.24), channel_id=1, source_target_pairs={{0,6},{2,0},{4,2},{6,4},{1,7},{3,1},{5,3},{7,5},{8,14},{10,8},{12,... | collective-permute-start | bytes 3145736 | tf_op jit(solution)/shard_map/ppermute | solution.py:200
  87.4 33.6 %all-to-all-start.1 = ((bf16[16,128,128]{2,1,0:T(8,128)(2,1)}), bf16[16,128,128]{2,1,0:T(8,128)(2,1)}, u32[]{:S(2)}, u32[]{:S(2)}) async-start(bf16[16,128,128]{2,1,0:T(8,128)(2,1)} %copy-done.7), calls=%async_computation.1 | async-start | bytes 1048576 | tf_op jit(solution)/shard_map/all_to_all | solution.py:229
  101.4 12.3 %collective-permute-start.4 = (bf16[8,128,256]{2,1,0:T(8,128)(2,1)}, bf16[8,128,256]{2,1,0:T(8,128)(2,1)}, u32[]{:S(2)}, u32[]{:S(2)}) collective-permute-start(bf16[8,128,256]{2,1,0:T(8,128)(2,1)} %slice.41), channel_id=1, source_target_pairs={{0,2},{2,4},{4,6},{6,0},{1,3},{3,5},{5,7},{7,1},{8,10},{10,12},{12... | collective-permute-start | bytes 1572872 | tf_op jit(solution)/shard_map/ppermute | solution.py:200
  102.5 13.1 %collective-permute-start.5 = (bf16[8,128,256]{2,1,0:T(8,128)(2,1)}, bf16[8,128,256]{2,1,0:T(8,128)(2,1)}, u32[]{:S(2)}, u32[]{:S(2)}) collective-permute-start(bf16[8,128,256]{2,1,0:T(8,128)(2,1)} %slice.42), channel_id=1, source_target_pairs={{0,6},{2,0},{4,2},{6,4},{1,7},{3,1},{5,3},{7,5},{8,14},{10,8},{12,... | collective-permute-start | bytes 1572872 | tf_op jit(solution)/shard_map/ppermute | solution.py:200
  105.0 17.3 %collective-permute-start = (bf16[16,128,256]{2,1,0:T(8,128)(2,1)}, bf16[16,128,256]{2,1,0:T(8,128)(2,1)}, u32[]{:S(2)}, u32[]{:S(2)}) collective-permute-start(bf16[16,128,256]{2,1,0:T(8,128)(2,1)} %bitcast.25), channel_id=1, source_target_pairs={{0,1},{1,0},{2,3},{3,2},{4,5},{5,4},{6,7},{7,6},{8,9},{9,8},{10,11... | collective-permute-start | bytes 3145736 | tf_op jit(solution)/shard_map/ppermute | solution.py:200
  108.2 14.1 %collective-permute-start.2 = (bf16[16,128,256]{2,1,0:T(8,128)(2,1)S(1)}, bf16[16,128,256]{2,1,0:T(8,128)(2,1)}, u32[]{:S(2)}, u32[]{:S(2)}) collective-permute-start(bf16[16,128,256]{2,1,0:T(8,128)(2,1)S(1)} %collective-permute-done.1.refs_2_), channel_id=1, source_target_pairs={{0,1},{1,0},{2,3},{3,2},{4,5},{5,4},{6,7},{7,6},{8,9},{9,8},{10,11... | collective-permute-start | bytes 3145736 | tf_op jit(solution)/shard_map/ppermute | solution.py:200
  108.5 13.8 %collective-permute-start.7 = (bf16[16,128,256]{2,1,0:T(8,128)(2,1)S(1)}, bf16[16,128,256]{2,1,0:T(8,128)(2,1)}, u32[]{:S(2)}, u32[]{:S(2)}) collective-permute-start(bf16[16,128,256]{2,1,0:T(8,128)(2,1)S(1)} %collective-permute-done.3.refs_6_), channel_id=1, source_target_pairs={{0,1},{1,0},{2,3},{3,2},{4,5},{5,4},{6,7},{7,6},{8,9},{9,8},{10,11... | collective-permute-start | bytes 3145736 | tf_op jit(solution)/shard_map/ppermute | solution.py:200
  117.5 6.2 %collective-permute-start.6 = (bf16[16,128,256]{2,1,0:T(8,128)(2,1)}, bf16[16,128,256]{2,1,0:T(8,128)(2,1)}, u32[]{:S(2)}, u32[]{:S(2)}) collective-permute-start(bf16[16,128,256]{2,1,0:T(8,128)(2,1)} %constant_dynamic-update-slice_fusion.refs_4_), channel_id=1, source_target_pairs={{0,1},{1,0},{2,3},{3,2},{4,5},{5,4},{6,7},{7,6},{8,9},{9,8},{10,11... | collective-permute-start | bytes 3145736 | tf_op jit(solution)/shard_map/ppermute | solution.py:200
  130.0 14.9 %collective-permute-start.11 = (bf16[128,2048]{1,0:T(8,128)(2,1)}, bf16[128,2048]{1,0:T(8,128)(2,1)}, u32[]{:S(2)}, u32[]{:S(2)}) collective-permute-start(bf16[128,2048]{1,0:T(8,128)(2,1)} %get-tuple-element.19.refs_0_), channel_id=1, source_target_pairs={{0,2},{2,4},{4,6},{6,0},{1,3},{3,5},{5,7},{7,1},{8,10},{10,12},{12... | collective-permute-start | bytes 1572872 | tf_op jit(solution)/shard_map/ppermute | solution.py:200
  130.0 15.9 %collective-permute-start.9 = (bf16[128,2048]{1,0:T(8,128)(2,1)}, bf16[128,2048]{1,0:T(8,128)(2,1)}, u32[]{:S(2)}, u32[]{:S(2)}) collective-permute-start(bf16[128,2048]{1,0:T(8,128)(2,1)} %get-tuple-element.19.refs_0_), channel_id=1, source_target_pairs={{0,6},{2,0},{4,2},{6,4},{1,7},{3,1},{5,3},{7,5},{8,14},{10,8},{12,... | collective-permute-start | bytes 1572872 | tf_op jit(solution)/shard_map/ppermute | solution.py:200
  145.8 8.2 %collective-permute-start.12 = (bf16[64,2048]{1,0:T(8,128)(2,1)S(1)}, bf16[64,2048]{1,0:T(8,128)(2,1)S(1)}, u32[]{:S(2)}, u32[]{:S(2)}) collective-permute-start(bf16[64,2048]{1,0:T(8,128)(2,1)S(1)} %slice.43), channel_id=1, source_target_pairs={{0,2},{2,4},{4,6},{6,0},{1,3},{3,5},{5,7},{7,1},{8,10},{10,12},{12... | collective-permute-start | bytes 786440 | tf_op jit(solution)/shard_map/ppermute | solution.py:200
  146.9 7.8 %collective-permute-start.13 = (bf16[64,2048]{1,0:T(8,128)(2,1)S(1)}, bf16[64,2048]{1,0:T(8,128)(2,1)S(1)}, u32[]{:S(2)}, u32[]{:S(2)}) collective-permute-start(bf16[64,2048]{1,0:T(8,128)(2,1)S(1)} %slice.44), channel_id=1, source_target_pairs={{0,6},{2,0},{4,2},{6,4},{1,7},{3,1},{5,3},{7,5},{8,14},{10,8},{12,... | collective-permute-start | bytes 786440 | tf_op jit(solution)/shard_map/ppermute | solution.py:200
  149.6 22.2 %collective-permute-start.8 = (bf16[128,2048]{1,0:T(8,128)(2,1)}, bf16[128,2048]{1,0:T(8,128)(2,1)}, u32[]{:S(2)}, u32[]{:S(2)}) collective-permute-start(bf16[128,2048]{1,0:T(8,128)(2,1)} %get-tuple-element.19.refs_0_), channel_id=1, source_target_pairs={{0,1},{1,0},{2,3},{3,2},{4,5},{5,4},{6,7},{7,6},{8,9},{9,8},{10,11... | collective-permute-start | bytes 1572872 | tf_op jit(solution)/shard_map/ppermute | solution.py:200
  151.2 20.6 %collective-permute-start.10 = (bf16[128,2048]{1,0:T(8,128)(2,1)}, bf16[128,2048]{1,0:T(8,128)(2,1)}, u32[]{:S(2)}, u32[]{:S(2)}) collective-permute-start(bf16[128,2048]{1,0:T(8,128)(2,1)} %collective-permute-done.9.refs_2_), channel_id=1, source_target_pairs={{0,1},{1,0},{2,3},{3,2},{4,5},{5,4},{6,7},{7,6},{8,9},{9,8},{10,11... | collective-permute-start | bytes 1572872 | tf_op jit(solution)/shard_map/ppermute | solution.py:200
  151.2 20.6 %collective-permute-start.15 = (bf16[128,2048]{1,0:T(8,128)(2,1)}, bf16[128,2048]{1,0:T(8,128)(2,1)}, u32[]{:S(2)}, u32[]{:S(2)}) collective-permute-start(bf16[128,2048]{1,0:T(8,128)(2,1)} %collective-permute-done.11.refs_6_), channel_id=1, source_target_pairs={{0,1},{1,0},{2,3},{3,2},{4,5},{5,4},{6,7},{7,6},{8,9},{9,8},{10,11... | collective-permute-start | bytes 1572872 | tf_op jit(solution)/shard_map/ppermute | solution.py:200
  155.5 16.4 %collective-permute-start.14 = (bf16[128,2048]{1,0:T(8,128)(2,1)}, bf16[128,2048]{1,0:T(8,128)(2,1)}, u32[]{:S(2)}, u32[]{:S(2)}) collective-permute-start(bf16[128,2048]{1,0:T(8,128)(2,1)} %constant_dynamic-update-slice_fusion.2.refs_4_), channel_id=1, source_target_pairs={{0,1},{1,0},{2,3},{3,2},{4,5},{5,4},{6,7},{7,6},{8,9},{9,8},{10,11... | collective-permute-start | bytes 1572872 | tf_op jit(solution)/shard_map/ppermute | solution.py:200
  177.4 4.4 %collective-permute-start.16 = (bf16[128,512]{1,0:T(8,128)(2,1)S(1)}, bf16[128,512]{1,0:T(8,128)(2,1)S(1)}, u32[]{:S(2)}, u32[]{:S(2)}) collective-permute-start(bf16[128,512]{1,0:T(8,128)(2,1)S(1)} %get-tuple-element.22), channel_id=1, source_target_pairs={{0,8},{8,0},{1,9},{9,1},{2,10},{10,2},{3,11},{11,3},{4,12},{12,4},... | collective-permute-start | bytes 393224 | tf_op jit(solution)/shard_map/ppermute | solution.py:200
  184.8 5.7 %collective-permute-start.19 = (bf16[128,2048]{1,0:T(8,128)(2,1)S(1)}, bf16[128,2048]{1,0:T(8,128)(2,1)S(1)}, u32[]{:S(2)}, u32[]{:S(2)}) collective-permute-start(bf16[128,2048]{1,0:T(8,128)(2,1)S(1)} %get-tuple-element.28), channel_id=1, source_target_pairs={{0,1},{1,0},{2,3},{3,2},{4,5},{5,4},{6,7},{7,6},{8,9},{9,8},{10,11... | collective-permute-start | bytes 1572872 | tf_op jit(solution)/shard_map/ppermute | solution.py:200
  190.4 3.8 %collective-permute-start.18 = (bf16[128,2048]{1,0:T(8,128)(2,1)S(1)}, bf16[128,2048]{1,0:T(8,128)(2,1)S(1)}, u32[]{:S(2)}, u32[]{:S(2)}) collective-permute-start(bf16[128,2048]{1,0:T(8,128)(2,1)S(1)} %get-tuple-element.26), channel_id=1, source_target_pairs={{0,1},{1,0},{2,3},{3,2},{4,5},{5,4},{6,7},{7,6},{8,9},{9,8},{10,11... | collective-permute-start | bytes 1572872 | tf_op jit(solution)/shard_map/ppermute | solution.py:200
  190.7 22.2 %copy-start.2 = (f32[128,2048]{1,0:T(8,128)S(1)}, f32[128,2048]{1,0:T(8,128)}, u32[]{:S(2)}) copy-start(f32[128,2048]{1,0:T(8,128)} %copy-done.1) | copy-start | bytes 3145732
  190.7 8.7 %collective-permute-start.20 = (bf16[64,2048]{1,0:T(8,128)(2,1)S(1)}, bf16[64,2048]{1,0:T(8,128)(2,1)S(1)}, u32[]{:S(2)}, u32[]{:S(2)}) collective-permute-start(bf16[64,2048]{1,0:T(8,128)(2,1)S(1)} %get-tuple-element.33), channel_id=1, source_target_pairs={{0,2},{2,4},{4,6},{6,0},{1,3},{3,5},{5,7},{7,1},{8,10},{10,12},{12... | collective-permute-start | bytes 786440 | tf_op jit(solution)/shard_map/ppermute | solution.py:200
  192.0 7.7 %collective-permute-start.22 = (bf16[128,2048]{1,0:T(8,128)(2,1)S(1)}, bf16[128,2048]{1,0:T(8,128)(2,1)S(1)}, u32[]{:S(2)}, u32[]{:S(2)}) collective-permute-start(bf16[128,2048]{1,0:T(8,128)(2,1)S(1)} %get-tuple-element.30), channel_id=1, source_target_pairs={{0,1},{1,0},{2,3},{3,2},{4,5},{5,4},{6,7},{7,6},{8,9},{9,8},{10,11... | collective-permute-start | bytes 1572872 | tf_op jit(solution)/shard_map/ppermute | solution.py:200
  192.7 10.3 %collective-permute-start.17 = (bf16[128,2048]{1,0:T(8,128)(2,1)S(1)}, bf16[128,2048]{1,0:T(8,128)(2,1)S(1)}, u32[]{:S(2)}, u32[]{:S(2)}) collective-permute-start(bf16[128,2048]{1,0:T(8,128)(2,1)S(1)} %get-tuple-element.24), channel_id=1, source_target_pairs={{0,1},{1,0},{2,3},{3,2},{4,5},{5,4},{6,7},{7,6},{8,9},{9,8},{10,11... | collective-permute-start | bytes 1572872 | tf_op jit(solution)/shard_map/ppermute | solution.py:200
  192.7 7.4 %collective-permute-start.23 = (bf16[64,2048]{1,0:T(8,128)(2,1)S(1)}, bf16[64,2048]{1,0:T(8,128)(2,1)S(1)}, u32[]{:S(2)}, u32[]{:S(2)}) collective-permute-start(bf16[64,2048]{1,0:T(8,128)(2,1)S(1)} %get-tuple-element.34), channel_id=1, source_target_pairs={{0,6},{2,0},{4,2},{6,4},{1,7},{3,1},{5,3},{7,5},{8,14},{10,8},{12,... | collective-permute-start | bytes 786440 | tf_op jit(solution)/shard_map/ppermute | solution.py:200
  199.6 13.4 %collective-permute-start.21 = (bf16[128,2048]{1,0:T(8,128)(2,1)S(1)}, bf16[128,2048]{1,0:T(8,128)(2,1)S(1)}, u32[]{:S(2)}, u32[]{:S(2)}) collective-permute-start(bf16[128,2048]{1,0:T(8,128)(2,1)S(1)} %add_convert_fusion.2), channel_id=1, source_target_pairs={{0,2},{2,4},{4,6},{6,0},{1,3},{3,5},{5,7},{7,1},{8,10},{10,12},{12... | collective-permute-start | bytes 1572872 | tf_op jit(solution)/shard_map/ppermute | solution.py:200
  200.3 12.7 %collective-permute-start.24 = (bf16[128,2048]{1,0:T(8,128)(2,1)S(1)}, bf16[128,2048]{1,0:T(8,128)(2,1)S(1)}, u32[]{:S(2)}, u32[]{:S(2)}) collective-permute-start(bf16[128,2048]{1,0:T(8,128)(2,1)S(1)} %add_convert_fusion.1), channel_id=1, source_target_pairs={{0,6},{2,0},{4,2},{6,4},{1,7},{3,1},{5,3},{7,5},{8,14},{10,8},{12,... | collective-permute-start | bytes 1572872 | tf_op jit(solution)/shard_map/ppermute | solution.py:200
  (10 other events, 18.6 us)
Sparse Core Ops, SparseCore 0:
  9.8 66.2 all-gather.4
  78.5 89.5 all-gather.6
